TPU v7x, 128 devices: a whole 4x4x4 slice. The times are simulated.
128 devices in a mesh: gx: 8 (over z_lo, y), gy: 8 (over x, core), gz: 2 (over z_hi).
Axes of the slice: x: 4, y: 4, z: 4 (z_hi: 2, z_lo: 2; z = z_hi * 2 + z_lo), core: 2. Of those that a mesh axis runs over, the one named last changes fastest.
Arguments:
- features: float32 [192, 192, 1536], P('gx', 'gy', 'gz'), may hold values from -6 to 6
- cotangent: float32 [192, 192, 1536], P('gx', 'gy', 'gz'), may hold values from -6 to 6
- skip_weight: float32 [32, 32], replicated, may hold values from -1 to 1
- bias_vector: float32 [32], replicated, may hold values from -3 to 3
- mode_factors: float32 [3, 3, 16, 64], replicated, may hold values from -4 to 4
- in_factors: float32 [3, 32, 64], replicated, may hold values from -1 to 1
- out_factors: float32 [3, 64, 32], replicated, may hold values from -0.75 to 0.75
Outputs:
- output: float32 [192, 192, 1536], P('gx', 'gy', 'gz')
- grad_skip: float32 [32, 32], replicated
- grad_bias: float32 [32], replicated
- grad_modes: float32 [3, 3, 16, 64], replicated
- grad_in: float32 [3, 32, 64], replicated
- grad_out: float32 [3, 64, 32], replicated
All inputs are finite; a program needn't handle non-finite values.
Results may differ from a plain program's by a relative error of at most 0.0003.
Values sent between devices are 32-bit elements; how exact they have to be, the bound alone decides.
A program may use at most 256 MiB of HBM per device.

v0:
```python
import math

import jax
import jax.numpy as jnp
from jax import lax
from jax.sharding import PartitionSpec as P

HIGHEST = lax.Precision.HIGHEST


def with_halo(cells, sides, width):
    for axis, dim in sides:
        count = lax.axis_size(axis)
        ends = count - 1
        head = lax.slice_in_dim(cells, 0, width, axis=dim)
        tail = lax.slice_in_dim(cells, cells.shape[dim] - width, cells.shape[dim], axis=dim)
        cells = jnp.concatenate(
            [
                lax.ppermute(tail, axis, [(i, (i + 1) % count) for i in range(ends)]),
                cells,
                lax.ppermute(head, axis, [((i + 1) % count, i) for i in range(ends)]),
            ],
            axis=dim,
        )
    return cells


def basis_table(length, modes):
    half_count = modes // 2
    mode_rows = jnp.arange(modes)
    frequency = jnp.where(mode_rows < half_count, mode_rows, mode_rows - half_count + 1).astype(
        jnp.float32
    )
    positions = jnp.arange(length).astype(jnp.float32)
    phases = 2.0 * math.pi / length * frequency[:, None] * positions[None, :]
    is_cosine = (mode_rows < half_count)[:, None]
    return jnp.where(is_cosine, jnp.cos(phases), jnp.sin(phases)) * math.sqrt(2.0 / length)


def spectral(grid, factor_modes, factor_in, factor_out):
    length = grid.shape[0]
    table = basis_table(length, factor_modes.shape[1])
    coeffs = jnp.einsum("ax,xyzi->ayzi", table, grid, precision=HIGHEST)
    coeffs = jnp.einsum("by,ayzi->abzi", table, coeffs, precision=HIGHEST)
    coeffs = jnp.einsum("cz,abzi->abci", table, coeffs, precision=HIGHEST)
    ranked = jnp.einsum("abci,ir->abcr", coeffs, factor_in, precision=HIGHEST)
    weights = (
        factor_modes[0][:, None, None, :]
        * factor_modes[1][None, :, None, :]
        * factor_modes[2][None, None, :, :]
    )
    result = jnp.einsum("abcr,ro->abco", ranked * weights, factor_out, precision=HIGHEST)
    result = jnp.einsum("ax,abco->xbco", table, result, precision=HIGHEST)
    result = jnp.einsum("by,xbco->xyco", table, result, precision=HIGHEST)
    return jnp.einsum("cz,xyco->xyzo", table, result, precision=HIGHEST)


def upsample(block, factor):
    block = jnp.repeat(block, factor, axis=0)
    block = jnp.repeat(block, factor, axis=1)
    return jnp.repeat(block, factor, axis=2)


def coarsen(field, factor):
    shape = field.shape
    split = field.reshape(
        shape[0] // factor, factor, shape[1] // factor, factor, shape[2] // factor, factor, shape[3]
    )
    return jnp.mean(split, axis=(1, 3, 5))


def layer(params, fine_patch, half_grid, quarter_grid):
    skip_weight, bias_vector, mode_factors, in_factors, out_factors = params
    patch = fine_patch.shape[0]
    start = patch // 4
    preact = jnp.einsum("xyzi,io->xyzo", fine_patch, skip_weight, precision=HIGHEST) + bias_vector
    preact = preact + spectral(fine_patch, mode_factors[0], in_factors[0], out_factors[0])
    half_out = spectral(half_grid, mode_factors[1], in_factors[1], out_factors[1])
    half_out = half_out[
        start : start + patch // 2, start : start + patch // 2, start : start + patch // 2
    ]
    preact = preact + upsample(half_out, 2)
    quarter_out = spectral(quarter_grid, mode_factors[2], in_factors[2], out_factors[2])
    quarter_out = quarter_out[
        start : start + patch // 4, start : start + patch // 4, start : start + patch // 4
    ]
    preact = preact + upsample(quarter_out, 4)
    return jax.nn.gelu(preact)


def per_device(
    features, cotangent, skip_weight, bias_vector, mode_factors, in_factors, out_factors
):
    patch = features.shape[0]
    channels = skip_weight.shape[0]
    fine_patch = features.reshape(patch, patch, patch, channels)
    cot_patch = cotangent.reshape(patch, patch, patch, channels)
    half_own = coarsen(fine_patch, 2)
    half_grid = with_halo(half_own, (("gx", 0), ("gy", 1), ("gz", 2)), patch // 4)
    quarter_grid = with_halo(coarsen(half_own, 2), (("gx", 0), ("gy", 1), ("gz", 2)), patch // 4)
    total_cells = (
        lax.axis_size("gx") * lax.axis_size("gy") * lax.axis_size("gz") * patch * patch * patch
    )
    scale = 1.0 / math.sqrt(total_cells)
    params = (skip_weight, bias_vector, mode_factors, in_factors, out_factors)
    result, pullback = jax.vjp(
        lambda values: layer(values, fine_patch, half_grid, quarter_grid), params
    )
    grads = pullback(cot_patch * scale)[0]
    summed = lax.psum((grads[0], grads[1], grads[2], grads[3], grads[4]), ("gx", "gy", "gz"))
    return (
        result.reshape(patch, patch, patch * channels),
        summed[0],
        summed[1],
        summed[2],
        summed[3],
        summed[4],
    )


def solution(mesh):
    placed = (P("gx", "gy", "gz"), P("gx", "gy", "gz"), P(), P(), P(), P(), P())
    return jax.shard_map(
        per_device,
        mesh=mesh,
        in_specs=placed,
        out_specs=(P("gx", "gy", "gz"), P(), P(), P(), P(), P()),
        check_vma=False,
    )
```

profile of v0, /device:TPU:1, one launch (start us, length us, event | category | flops | bytes accessed | tf_op | source)
XLA Modules:
  0.0 549.0 jit_solution(11529056693796468882)
XLA Ops:
  7.2 8.1 %reshape_reshape.3 = f32[12,2,12,2,12,2,32]{6,5,4,3,2,1,0:T(2,128)} reshape(f32[24,24,768]{2,1,0:T(8,128)} %param.7) | data formatting | bytes 3538944 | tf_op jit(solution)/shard_map/reshape;reshape | solution.py:66
  15.3 7.6 %reduce_sum.183 = f32[12,12,12,32]{3,2,1,0:T(8,128)S(1)} reduce(f32[12,2,12,2,12,2,32]{6,5,4,3,2,1,0:T(2,128)} %reshape_reshape.3, f32[]{:T(128)} %constant.9.clone.1), dimensions={1,3,5}, to_apply=%region_0.0 | reduce | flops 387072 | bytes 1990660 | tf_op jit(solution)/shard_map/reduce_sum | solution.py:69
  28.8 5.3 collective-permute-start.6
  36.5 5.1 collective-permute-start
  49.4 12.1 %fusion.26 = f32[16,24,24,32]{3,0,2,1:T(8,128)S(1)} fusion(f32[24,24,24,32]{3,2,1,0:T(8,128)} %reshape.197, f32[24]{0:T(128)S(1)} %iota_convert_fusion.1, f32[16]{0:T(128)S(1)} %broadcast_multiply_fusion.6, pred[16]{0:T(512)(128)(4,1)S(1)} %iota_compare_fusion), kind=kOutput, calls=%fused_computation.29 | convolution fusion | flops 84935808 | bytes 2949296 | tf_op jit(solution)/shard_map/jvp(ax,xyzi->ayzi)/dot_general | solution.py:43
  61.5 6.3 %fusion.135 = f32[16,16,24,32]{3,1,2,0:T(8,128)S(1)} fusion(f32[16,24,24,32]{3,0,2,1:T(8,128)S(1)} %fusion.26, f32[24]{0:T(128)S(1)} %iota_convert_fusion.1, f32[16]{0:T(128)S(1)} %broadcast_multiply_fusion.6, pred[16]{0:T(512)(128)(4,1)S(1)} %iota_compare_fusion), kind=kOutput, calls=%fused_computation.136 | convolution fusion | flops 56624256 | bytes 1966256 | tf_op jit(solution)/shard_map/jvp(by,ayzi->abzi)/dot_general | solution.py:44
  82.9 6.7 %fusion.90 = f32[24,24,16,32]{3,1,2,0:T(8,128)} fusion(f32[24,16,16,32]{3,0,2,1:T(8,128)S(1)} %fusion.218, f32[24]{0:T(128)S(1)} %iota_convert_fusion.1, f32[16]{0:T(128)S(1)} %broadcast_multiply_fusion.6, pred[16]{0:T(512)(128)(4,1)S(1)} %iota_compare_fusion), kind=kOutput, calls=%fused_computation.95 | convolution fusion | flops 56624256 | bytes 1966256 | tf_op jit(solution)/shard_map/jvp(by,xbco->xyco)/dot_general | solution.py:54
  89.7 7.7 %fusion.183 = f32[24,24,24,32]{3,2,1,0:T(8,128)} fusion(f32[24,24,24,32]{3,2,1,0:T(8,128)S(1)} %bitcast.287, f32[32,32]{1,0:T(8,128)S(1)} %copy-done), kind=kOutput, calls=%fused_computation.180 | convolution fusion | flops 169869312 | bytes 3543040 | tf_op jit(solution)/shard_map/jvp(xyzi,io->xyzo)/dot_general | solution.py:76
  98.0 5.7 %mul.638 = f32[24,24,24,32]{3,2,1,0:T(8,128)} reshape(f32[24,24,768]{2,1,0:T(8,128)} %broadcast_multiply_fusion) | data formatting | bytes 3538944 | tf_op jit(solution)/shard_map/mul | solution.py:109
  121.6 5.7 %collective-permute-start.10 = (f32[18,18,6,32]{3,0,2,1:T(8,128)S(1)}, f32[18,18,6,32]{3,0,2,1:T(8,128)S(1)}, u32[]{:S(2)}, u32[]{:S(2)}) collective-permute-start(f32[18,18,6,32]{3,0,2,1:T(8,128)S(1)} %pad_maximum_fusion.2), channel_id=1, source_target_pairs={{0,1},{2,3},{4,5},{6,7},{8,9},{10,11},{12,13},{14,15},{16,17},{18,... | collective-permute-start | bytes 746504 | tf_op jit(solution)/shard_map/ppermute | solution.py:19
  133.6 6.1 %collective-permute-start.4 = (f32[24,24,6,32]{3,1,2,0:T(8,128)S(1)}, f32[24,24,6,32]{3,1,2,0:T(8,128)S(1)}, u32[]{:S(2)}, u32[]{:S(2)}) collective-permute-start(f32[24,24,6,32]{3,1,2,0:T(8,128)S(1)} %copy.109), channel_id=1, source_target_pairs={{0,1},{2,3},{4,5},{6,7},{8,9},{10,11},{12,13},{14,15},{16,17},{18,... | collective-permute-start | bytes 1327112 | tf_op jit(solution)/shard_map/ppermute | solution.py:19
  139.7 15.2 %collective-permute-done.11 = f32[18,18,6,32]{3,0,2,1:T(8,128)S(1)} collective-permute-done((f32[18,18,6,32]{3,0,2,1:T(8,128)S(1)}, f32[18,18,6,32]{3,0,2,1:T(8,128)S(1)}, u32[]{:S(2)}, u32[]{:S(2)}) %collective-permute-start.11) | collective-permute-done | bytes 248864 | tf_op jit(solution)/shard_map/ppermute | solution.py:21
  176.1 4.4 fusion.120
  184.6 7.3 %collective-permute-done.5 = f32[24,24,6,32]{3,1,2,0:T(8,128)S(1)} collective-permute-done((f32[24,24,6,32]{3,1,2,0:T(8,128)S(1)}, f32[24,24,6,32]{3,1,2,0:T(8,128)S(1)}, u32[]{:S(2)}, u32[]{:S(2)}) %collective-permute-start.5) | collective-permute-done | bytes 442400 | tf_op jit(solution)/shard_map/ppermute | solution.py:21
  194.2 6.6 %fusion.6 = f32[16,24,24,32]{3,0,2,1:T(8,128)S(1)} fusion(f32[24,24,6,32]{3,0,2,1:T(8,128)S(1)} %copy.112, f32[24,6,12,32]{3,0,2,1:T(8,128)S(1)} %collective-permute-done.3, f32[6,12,12,32]{3,0,2,1:T(8,128)} %collective-permute-done.1, f32[12,12,12,32]{3,0,2,1:T(8,128)S(1)} %copy_multiply_fusion, f32[6,12,12,32]{3,0,2,1:T(8,128)} %collective-permute-done, ...), kind=kOutput, calls=%fused_computation.8 | convolution fusion | flops 87590016 | bytes 2949296 | tf_op jit(solution)/shard_map/jvp(ax,xyzi->ayzi)/dot_general | solution.py:43
  200.9 6.7 %fusion.138 = f32[16,16,24,32]{3,1,2,0:T(8,128)S(1)} fusion(f32[16,24,24,32]{3,0,2,1:T(8,128)S(1)} %fusion.6, f32[24]{0:T(128)S(1)} %copy-done.27, f32[16]{0:T(128)S(1)} %copy-done.29, pred[16]{0:T(512)(128)(4,1)S(1)} %copy-done.23), kind=kOutput, calls=%fused_computation.137 | convolution fusion | flops 56624256 | bytes 1966256 | tf_op jit(solution)/shard_map/jvp(by,ayzi->abzi)/dot_general | solution.py:44
  219.9 5.9 %fusion.93 = f32[24,24,16,32]{3,1,2,0:T(8,128)S(1)} fusion(f32[24,16,16,32]{3,0,2,1:T(8,128)S(1)} %fusion.211, f32[24]{0:T(128)S(1)} %copy-done.27, f32[16]{0:T(128)S(1)} %copy-done.29, pred[16]{0:T(512)(128)(4,1)S(1)} %copy-done.23), kind=kOutput, calls=%fused_computation.96 | convolution fusion | flops 56624256 | bytes 1966256 | tf_op jit(solution)/shard_map/jvp(by,xbco->xyco)/dot_general | solution.py:54
  225.9 6.9 %fusion.80 = f32[24,24,24,32]{3,2,1,0:T(8,128)S(1)} fusion(f32[24,24,16,32]{3,1,2,0:T(8,128)S(1)} %fusion.93, f32[24]{0:T(128)S(1)} %copy-done.27, f32[16]{0:T(128)S(1)} %copy-done.29, pred[16]{0:T(512)(128)(4,1)S(1)} %copy-done.23), kind=kOutput, calls=%fused_computation.89 | convolution fusion | flops 84935808 | bytes 2949296 | tf_op jit(solution)/shard_map/jvp(cz,xyco->xyzo)/dot_general | solution.py:55
  238.0 4.8 broadcast_in_dim.154
  242.8 22.4 %fusion.376 = (f32[32]{0:T(128)}, f32[24,24,24,32]{3,2,1,0:T(8,128)}, f32[24,24,24,32]{3,2,1,0:T(8,128)}) fusion(f32[24,24,24,32]{3,2,1,0:T(8,128)} %mul.638, f32[24,24,24,32]{3,2,1,0:T(8,128)} %bitcast.294, f32[24,24,24,32]{3,2,1,0:T(8,128)} %bitcast.295, f32[24]{0:T(128)S(1)} %copy-done.27, f32[16]{0:T(128)S(1)} %copy-done.29, ...), kind=kOutput, calls=%fused_computation.365 | convolution fusion | flops 95994976 | bytes 11796912 | tf_op jit(solution)/shard_map/jvp(cz,xyco->xyzo)/dot_general | solution.py:55
  265.3 15.3 %convolution_bitcast_fusion = f32[32,32]{0,1:T(8,128)} fusion(f32[24,24,24,32]{3,2,1,0:T(8,128)} %get-tuple-element.54, f32[24,24,24,32]{3,2,1,0:T(8,128)} %reshape.197), kind=kOutput, calls=%fused_computation.152 | convolution fusion | flops 169869312 | bytes 3543040 | tf_op jit(solution)/shard_map/transpose(jvp(xyzi,io->xyzo))/dot_general | solution.py:76
  280.6 5.5 fusion.96
  286.1 4.6 fusion.144
  295.1 4.7 fusion.162
  299.8 4.9 multiply_reduce_fusion.1
  304.7 12.7 %reduce_sum.202 = f32[24,24,12,32]{3,2,1,0:T(8,128)} reduce(f32[24,24,12,2,32]{4,3,2,1,0:T(2,128)} %bitcast.284, f32[]{:T(128)} %constant.9.clone.1), dimensions={3}, to_apply=%region_12.13 | reduce | flops 221184 | bytes 2654212 | tf_op jit(solution)/shard_map/transpose(jvp())/reduce_sum | solution.py:61
  317.4 4.8 reduce_sum.203
  327.2 4.6 fusion.141
  344.5 9.2 %reduce_sum.189 = f32[24,24,6,32]{3,2,1,0:T(8,128)} reduce(f32[24,24,6,4,32]{4,3,2,1,0:T(4,128)} %bitcast.285, f32[]{:T(128)} %constant.9.clone.1), dimensions={3}, to_apply=%region_5.6 | reduce | flops 331776 | bytes 2211844 | tf_op jit(solution)/shard_map/transpose(jvp())/reduce_sum | solution.py:61
  365.2 4.5 fusion.156
  385.9 5.6 %reshape.204 = f32[24,24,768]{2,1,0:T(8,128)} reshape(f32[24,24,24,32]{3,2,1,0:T(8,128)} %get-tuple-element.55) | data formatting | bytes 3538944 | tf_op jit(solution)/shard_map/reshape | solution.py:112
  391.5 143.6 %all-reduce.23.cloned.1.call-done = (f32[32,32]{0,1:T(8,128)}, f32[32]{0:T(128)}, f32[3,3,16,64]{3,2,1,0:T(8,128)}, f32[3,32,64]{2,1,0:T(8,128)}, f32[3,64,32]{1,2,0:T(8,128)}) async-done(((f32[32,32]{0,1:T(8,128)}, f32[32]{0:T(128)}, f32[3,3,16,64]{3,2,1,0:T(8,128)}, f32[3,32,64]{2,1,0:T(8,128)}, f32[3,64,32]{1,2,0:T(8,128)}), (f32[32,32]{0,1:T(8,128)}, f32[32]{0:T(128)}, f32[3,3,16,64]{3,2,1,0:T(8,128)}, ...) | async-done | bytes 90256 | tf_op jit(solution)/shard_map/psum | solution.py:110
  (217 shorter events, 157.0 us)
Async XLA Ops:
  7.2 82.5 %copy-start = (f32[32,32]{1,0:T(8,128)S(1)}, f32[32,32]{1,0:T(8,128)}, u32[]{:S(2)}) copy-start(f32[32,32]{1,0:T(8,128)} %param.9) | copy-start | bytes 12292
  7.2 527.9 %all-reduce.23.cloned.1.call-start = ((), (), s32[]{:S(2)}) async-start(), calls=%async_computation | async-start | bytes 377856 | tf_op jit(solution)/shard_map/psum | solution.py:110
  25.0 16.7 %copy-start.18 = (f32[24,24,768]{2,1,0:T(8,128)S(1)}, f32[24,24,768]{2,1,0:T(8,128)}, u32[]{:S(2)}) copy-start(f32[24,24,768]{2,1,0:T(8,128)} %param.7) | copy-start | bytes 5308420
  27.5 76.3 %collective-permute-start.7 = (f32[6,6,6,32]{3,0,2,1:T(8,128)}, f32[6,6,6,32]{3,0,2,1:T(8,128)}, u32[]{:S(2)}, u32[]{:S(2)}) collective-permute-start(f32[6,6,6,32]{3,0,2,1:T(8,128)} %broadcast_multiply_fusion.1), channel_id=1, source_target_pairs={{16,0},{32,16},{48,32},{64,48},{80,64},{96,80},{112,96},{17,1},{33... | collective-permute-start | bytes 82952 | tf_op jit(solution)/shard_map/ppermute | solution.py:21
  28.8 75.0 %collective-permute-start.6 = (f32[6,6,6,32]{3,0,2,1:T(8,128)}, f32[6,6,6,32]{3,0,2,1:T(8,128)}, u32[]{:S(2)}, u32[]{:S(2)}) collective-permute-start(f32[6,6,6,32]{3,0,2,1:T(8,128)} %broadcast_multiply_fusion.1), channel_id=1, source_target_pairs={{0,16},{16,32},{32,48},{48,64},{64,80},{80,96},{96,112},{1,17},{17... | collective-permute-start | bytes 82952 | tf_op jit(solution)/shard_map/ppermute | solution.py:19
  35.2 76.5 %collective-permute-start.1 = (f32[6,12,12,32]{3,0,2,1:T(8,128)}, f32[6,12,12,32]{3,0,2,1:T(8,128)}, u32[]{:S(2)}, u32[]{:S(2)}) collective-permute-start(f32[6,12,12,32]{3,0,2,1:T(8,128)} %get-tuple-element.61), channel_id=1, source_target_pairs={{16,0},{32,16},{48,32},{64,48},{80,64},{96,80},{112,96},{17,1},{33... | collective-permute-start | bytes 331784 | tf_op jit(solution)/shard_map/ppermute | solution.py:21
  36.5 75.2 %collective-permute-start = (f32[6,12,12,32]{3,0,2,1:T(8,128)}, f32[6,12,12,32]{3,0,2,1:T(8,128)}, u32[]{:S(2)}, u32[]{:S(2)}) collective-permute-start(f32[6,12,12,32]{3,0,2,1:T(8,128)} %get-tuple-element.60), channel_id=1, source_target_pairs={{0,16},{16,32},{32,48},{48,64},{64,80},{80,96},{96,112},{1,17},{17... | collective-permute-start | bytes 331784 | tf_op jit(solution)/shard_map/ppermute | solution.py:19
  41.6 41.3 %copy-start.22 = (pred[16]{0:T(512)(128)(4,1)}, pred[16]{0:T(512)(128)(4,1)S(1)}, u32[]{:S(2)}) copy-start(pred[16]{0:T(512)(128)(4,1)S(1)} %iota_compare_fusion) | copy-start | bytes 52
  41.7 41.2 %copy-start.26 = (f32[24]{0:T(128)}, f32[24]{0:T(128)S(1)}, u32[]{:S(2)}) copy-start(f32[24]{0:T(128)S(1)} %iota_convert_fusion.1) | copy-start | bytes 292
  41.7 41.2 %copy-start.28 = (f32[16]{0:T(128)}, f32[16]{0:T(128)S(1)}, u32[]{:S(2)}) copy-start(f32[16]{0:T(128)S(1)} %broadcast_multiply_fusion.6) | copy-start | bytes 196
  49.3 21.4 %copy-start.37 = (f32[16,64]{1,0:T(8,128)}, f32[16,64]{1,0:T(8,128)S(1)}, u32[]{:S(2)}) copy-start(f32[16,64]{1,0:T(8,128)S(1)} %get-tuple-element.62) | copy-start | bytes 12292
  49.3 21.4 %copy-start.43 = (f32[16,64]{1,0:T(8,128)}, f32[16,64]{1,0:T(8,128)S(1)}, u32[]{:S(2)}) copy-start(f32[16,64]{1,0:T(8,128)S(1)} %get-tuple-element.68) | copy-start | bytes 12292
  49.3 21.4 %copy-start.34 = (f32[16,64]{1,0:T(8,128)}, f32[16,64]{1,0:T(8,128)S(1)}, u32[]{:S(2)}) copy-start(f32[16,64]{1,0:T(8,128)S(1)} %get-tuple-element.67) | copy-start | bytes 12292
  49.3 48.0 %copy-start.45 = (f32[16,64]{1,0:T(8,128)}, f32[16,64]{1,0:T(8,128)S(1)}, u32[]{:S(2)}) copy-start(f32[16,64]{1,0:T(8,128)S(1)} %get-tuple-element.63) | copy-start | bytes 12292
  49.3 48.0 %copy-start.47 = (f32[16,64]{1,0:T(8,128)}, f32[16,64]{1,0:T(8,128)S(1)}, u32[]{:S(2)}) copy-start(f32[16,64]{1,0:T(8,128)S(1)} %get-tuple-element.70) | copy-start | bytes 12292
  49.3 48.0 %copy-start.39 = (f32[16,64]{1,0:T(8,128)}, f32[16,64]{1,0:T(8,128)S(1)}, u32[]{:S(2)}) copy-start(f32[16,64]{1,0:T(8,128)S(1)} %get-tuple-element.65) | copy-start | bytes 12292
  49.3 48.0 %copy-start.41 = (f32[16,64]{1,0:T(8,128)}, f32[16,64]{1,0:T(8,128)S(1)}, u32[]{:S(2)}) copy-start(f32[16,64]{1,0:T(8,128)S(1)} %get-tuple-element.66) | copy-start | bytes 12292
  80.0 9.6 %slice-start = ((s8[7077888]{0:T(1024)(128)(4,1)}), s8[4194304]{0:T(1024)(128)(4,1)S(1)}, s32[]{:S(2)}) async-start(s8[7077888]{0:T(1024)(128)(4,1)} %bitcast.286), calls=%async_computation.1 | async-start | bytes 8388608
  82.9 6.7 %slice-start.1 = ((s8[7077888]{0:T(1024)(128)(4,1)}), s8[2883584]{0:T(1024)(128)(4,1)S(1)}, s32[]{:S(2)}) async-start(s8[7077888]{0:T(1024)(128)(4,1)} %bitcast.286), calls=%async_computation.2 | async-start | bytes 5767168
  98.0 82.5 %copy-start.53 = (f32[18]{0:T(128)}, f32[18]{0:T(128)S(1)}, u32[]{:S(2)}) copy-start(f32[18]{0:T(128)S(1)} %iota_convert_fusion) | copy-start | bytes 220
  104.9 14.3 %collective-permute-start.9 = (f32[18,6,6,32]{3,0,2,1:T(8,128)S(1)}, f32[18,6,6,32]{3,0,2,1:T(8,128)S(1)}, u32[]{:S(2)}, u32[]{:S(2)}) collective-permute-start(f32[18,6,6,32]{3,0,2,1:T(8,128)S(1)} %pad_maximum_fusion.3), channel_id=1, source_target_pairs={{2,0},{4,2},{6,4},{8,6},{10,8},{12,10},{14,12},{3,1},{5,3},{7,5},{... | collective-permute-start | bytes 248840 | tf_op jit(solution)/shard_map/ppermute | solution.py:21
  108.6 10.5 %collective-permute-start.8 = (f32[18,6,6,32]{3,0,2,1:T(8,128)S(1)}, f32[18,6,6,32]{3,0,2,1:T(8,128)S(1)}, u32[]{:S(2)}, u32[]{:S(2)}) collective-permute-start(f32[18,6,6,32]{3,0,2,1:T(8,128)S(1)} %pad_maximum_fusion.3), channel_id=1, source_target_pairs={{0,2},{2,4},{4,6},{6,8},{8,10},{10,12},{12,14},{1,3},{3,5},{5,7},{... | collective-permute-start | bytes 248840 | tf_op jit(solution)/shard_map/ppermute | solution.py:19
  113.5 14.7 %collective-permute-start.3 = (f32[24,6,12,32]{3,0,2,1:T(8,128)S(1)}, f32[24,6,12,32]{3,0,2,1:T(8,128)S(1)}, u32[]{:S(2)}, u32[]{:S(2)}) collective-permute-start(f32[24,6,12,32]{3,0,2,1:T(8,128)S(1)} %get-tuple-element.59), channel_id=1, source_target_pairs={{2,0},{4,2},{6,4},{8,6},{10,8},{12,10},{14,12},{3,1},{5,3},{7,5},{... | collective-permute-start | bytes 663560 | tf_op jit(solution)/shard_map/ppermute | solution.py:21
  115.4 13.6 %collective-permute-start.2 = (f32[24,6,12,32]{3,0,2,1:T(8,128)S(1)}, f32[24,6,12,32]{3,0,2,1:T(8,128)S(1)}, u32[]{:S(2)}, u32[]{:S(2)}) collective-permute-start(f32[24,6,12,32]{3,0,2,1:T(8,128)S(1)} %get-tuple-element.58), channel_id=1, source_target_pairs={{0,2},{2,4},{4,6},{6,8},{8,10},{10,12},{12,14},{1,3},{3,5},{5,7},{... | collective-permute-start | bytes 663560 | tf_op jit(solution)/shard_map/ppermute | solution.py:19
  119.1 61.4 %copy-start.55 = (f32[16]{0:T(128)}, f32[16]{0:T(128)S(1)}, u32[]{:S(2)}) copy-start(f32[16]{0:T(128)S(1)} %broadcast_multiply_fusion.5) | copy-start | bytes 196
  120.3 34.5 %collective-permute-start.11 = (f32[18,18,6,32]{3,0,2,1:T(8,128)S(1)}, f32[18,18,6,32]{3,0,2,1:T(8,128)S(1)}, u32[]{:S(2)}, u32[]{:S(2)}) collective-permute-start(f32[18,18,6,32]{3,0,2,1:T(8,128)S(1)} %pad_maximum_fusion.2), channel_id=1, source_target_pairs={{1,0},{3,2},{5,4},{7,6},{9,8},{11,10},{13,12},{15,14},{17,16},{19,... | collective-permute-start | bytes 746504 | tf_op jit(solution)/shard_map/ppermute | solution.py:21
  121.6 34.5 %collective-permute-start.10 = (f32[18,18,6,32]{3,0,2,1:T(8,128)S(1)}, f32[18,18,6,32]{3,0,2,1:T(8,128)S(1)}, u32[]{:S(2)}, u32[]{:S(2)}) collective-permute-start(f32[18,18,6,32]{3,0,2,1:T(8,128)S(1)} %pad_maximum_fusion.2), channel_id=1, source_target_pairs={{0,1},{2,3},{4,5},{6,7},{8,9},{10,11},{12,13},{14,15},{16,17},{18,... | collective-permute-start | bytes 746504 | tf_op jit(solution)/shard_map/ppermute | solution.py:19
  131.7 24.4 %copy-start.23 = (pred[16]{0:T(512)(128)(4,1)S(1)}, pred[16]{0:T(512)(128)(4,1)}, u32[]{:S(2)}) copy-start(pred[16]{0:T(512)(128)(4,1)} %copy-done.22) | copy-start | bytes 52
  131.7 60.1 %collective-permute-start.5 = (f32[24,24,6,32]{3,1,2,0:T(8,128)S(1)}, f32[24,24,6,32]{3,1,2,0:T(8,128)S(1)}, u32[]{:S(2)}, u32[]{:S(2)}) collective-permute-start(f32[24,24,6,32]{3,1,2,0:T(8,128)S(1)} %copy.110), channel_id=1, source_target_pairs={{1,0},{3,2},{5,4},{7,6},{9,8},{11,10},{13,12},{15,14},{17,16},{19,... | collective-permute-start | bytes 1327112 | tf_op jit(solution)/shard_map/ppermute | solution.py:21
  133.6 60.1 %collective-permute-start.4 = (f32[24,24,6,32]{3,1,2,0:T(8,128)S(1)}, f32[24,24,6,32]{3,1,2,0:T(8,128)S(1)}, u32[]{:S(2)}, u32[]{:S(2)}) collective-permute-start(f32[24,24,6,32]{3,1,2,0:T(8,128)S(1)} %copy.109), channel_id=1, source_target_pairs={{0,1},{2,3},{4,5},{6,7},{8,9},{10,11},{12,13},{14,15},{16,17},{18,... | collective-permute-start | bytes 1327112 | tf_op jit(solution)/shard_map/ppermute | solution.py:19
  265.3 15.3 %copy-start.2 = (f32[24,24,24,32]{3,2,1,0:T(8,128)S(1)}, f32[24,24,24,32]{3,2,1,0:T(8,128)}, u32[]{:S(2)}) copy-start(f32[24,24,24,32]{3,2,1,0:T(8,128)} %get-tuple-element.54) | copy-start | bytes 5308420
  385.9 156.1 %copy-start.1 = (f32[32,32]{1,0:T(8,128)S(1)}, f32[32,32]{1,0:T(8,128)}, u32[]{:S(2)}) copy-start(f32[32,32]{1,0:T(8,128)} %param.9) | copy-start | bytes 12292
  (41 other events, 146.7 us)
Sparse Core Ops, SparseCore 0:
  386.0 149.0 all-reduce.22
where the time goes:
time: 557 us; the launch traced here: 549 us
  matrix products  223 us (40%)
  waiting for transfers between devices  170 us (31%)
  other arithmetic  53 us (10%)
  local copies, waits for them, and re-layouts  47.9 us (9%)
  starting transfers between devices  39.9 us (7%)
  between operations  15.5 us (3%)
    psum x1, waiting for transfers between devices, per_device(): lax.psum((grads[0], grads[1], grads[2], grads[3], grads[4]), ('gx', 'gy',...  144 us
    dot_general x6, matrix products, spectral(): return jnp.einsum('cz,xyco->xyzo', table, result, precision=HIGHEST)  44 us
    dot_general x9, matrix products, spectral(): jnp.einsum('abcr,ro->abco', ranked * weights, factor_out, precision=HIGHEST)  35.3 us
    dot_general x6, matrix products, spectral(): result = jnp.einsum('by,xbco->xyco', table, result, precision=HIGHEST)  29.5 us
    ppermute x6, starting transfers between devices, with_halo(): lax.ppermute(tail, axis, [(i, (i + 1) % count) for i in range(ends)])  29 us
    ppermute x6, waiting for transfers between devices, with_halo(): lax.ppermute(head, axis, [((i + 1) % count, i) for i in range(ends)])  23.3 us
    dot_general x2, matrix products, layer(): jnp.einsum('xyzi,io->xyzo', fine_patch, skip_weight, precision=HIGHEST)  23 us
    dot_general x3, matrix products, spectral(): coeffs = jnp.einsum('ax,xyzi->ayzi', table, grid, precision=HIGHEST)  22.5 us
  transfers between devices with their start and end apart: 13, of which 7 were waited for; matrix products, arithmetic and copies ran while one was open for 19% of the time, Pallas kernels for 0%

commit v1 on v0

v1 whole, which is shorter than its diff:
```python
import math

import jax
import jax.numpy as jnp
import ml_dtypes
import numpy as np
from jax import lax
from jax.experimental import pallas as pl
from jax.experimental.pallas import tpu as pltpu
from jax.sharding import PartitionSpec as P

MESH = pl.DeviceIdType.MESH
BF = jnp.bfloat16
F32 = jnp.float32
CH, RK, MD, NP = 32, 64, 16, 24
NN = (((1,), (0,)), ((), ()))
NT = (((1,), (1,)), ((), ()))
TN = (((0,), (0,)), ((), ()))
PAY = 192


def basis(length):
    rows = np.arange(MD)
    freq = np.where(rows < MD // 2, rows, rows - MD // 2 + 1).astype(np.float64)
    phase = 2.0 * math.pi / length * freq[:, None] * np.arange(length)[None, :]
    wave = np.where((rows < MD // 2)[:, None], np.cos(phase), np.sin(phase))
    return wave * math.sqrt(2.0 / length)


def halves(x):
    x = np.asarray(x, np.float32)
    hi = x.astype(ml_dtypes.bfloat16)
    lo = (x - hi.astype(np.float32)).astype(ml_dtypes.bfloat16)
    return hi, lo


def left(x):
    hi, lo = halves(x)
    return np.concatenate([hi, hi, lo], axis=1)


def right(x):
    hi, lo = halves(x)
    return np.concatenate([hi, lo], axis=0)


def exact(x, times, axis):
    x = np.asarray(x, np.float32).astype(ml_dtypes.bfloat16)
    return np.concatenate([x] * times, axis=axis)


def channel_eye(b):
    return np.kron(b, np.eye(CH))


def make_tables():
    b24, b18 = basis(24), basis(18)
    pool = np.zeros((208, 12, 24))
    for j in range(2):
        for i in range(2):
            for r in range(36):
                x, y = i * 6 + r // 6, 2 * (j * 6 + r % 6)
                pool[(j * 2 + i) * 40 + r, x, y : y + 2] = 1 / 8
    for r in range(36):
        x, y = 2 * (r // 6), 4 * (r % 6)
        pool[160 + r, x : x + 2, y : y + 4] = 1 / 64
    pool = pool.reshape(208, 288)
    pair = channel_eye(np.kron(np.eye(4), np.ones((2, 1))))
    quad = np.zeros((24, 8))
    for z in range(24):
        quad[z, z // 4] = 1
    quad = channel_eye(quad)
    xy0 = np.kron(b24, b24)
    xy1 = np.zeros((256, 4, 4, 40))
    for j in range(4):
        for i in range(4):
            for r in range(36):
                xy1[:, j, i, r] = np.kron(b24[:, i * 6 + r // 6], b24[:, j * 6 + r % 6])
    xy2 = np.zeros((256, 368))
    for j in range(3):
        for i in range(3):
            for r in range(36):
                xy2[:, (j * 3 + i) * 40 + r] = np.kron(
                    b18[:, i * 6 + r // 6], b18[:, j * 6 + r % 6]
                )
    z0 = channel_eye(b24.T)
    z1s, z2s = [], []
    for gz in range(2):
        z1 = np.zeros((20, 16))
        z1[0:12] = b24[:, 6:18].T
        if gz == 0:
            z1[12:18] = b24[:, 18:24].T
        else:
            z1[14:20] = b24[:, 0:6].T
        z1s.append(right(channel_eye(z1)))
        z2 = np.zeros((16, 16))
        z2[0:6] = b18[:, 6:12].T
        z2[8:14] = b18[:, 12:18].T if gz == 0 else b18[:, 0:6].T
        z2s.append(right(channel_eye(z2)))
    z1c = channel_eye(b24[:, 6:18])
    z2c = channel_eye(np.repeat(b18[:, 6:12], 2, axis=1))
    c1 = b24[:, 6:18]
    c2 = np.repeat(b18[:, 6:12], 2, axis=1)
    xy12 = np.concatenate([np.kron(c1, c1), np.kron(c2, c2)], axis=0)
    return {
        "pool": exact(pool, 2, 1),
        "pair": exact(pair, 2, 0),
        "quad": exact(quad, 2, 0),
        "unpair": exact(pair.T, 2, 0),
        "xy0": left(xy0),
        "z0": right(z0),
        "z0t": right(z0.T),
        "inv": left(xy0.T),
        "xy1": left(xy1.reshape(256, 640)),
        "z1": np.concatenate(z1s, axis=0),
        "xy2": left(xy2),
        "z2": np.concatenate(z2s, axis=0),
        "z1c": right(z1c),
        "z2c": right(z2c),
        "xy12": left(xy12.T),
        "xy12t": left(xy12),
        "z2ct": right(z2c.T),
    }


TABLES = make_tables()
NAMES = list(TABLES)


def table_shape(name):
    rows, cols = TABLES[name].shape
    return (rows // 2 if name in ("z1", "z2") else rows), cols


def dot(a, b, dims=NN):
    return lax.dot_general(a, b, dims, preferred_element_type=F32)


def split(x):
    hi = x.astype(BF)
    return hi, (x - hi.astype(F32)).astype(BF)


def rows_cat(*parts):
    return jnp.concatenate(parts, axis=0)


def lanes_cat(*parts):
    return jnp.concatenate(parts, axis=1)


def iota(shape, dim):
    return lax.broadcasted_iota(jnp.int32, shape, dim)


def fold_lanes(x):
    total = x[:, 0:128]
    for k in range(1, x.shape[1] // 128):
        total = total + x[:, 128 * k : 128 * (k + 1)]
    return total + pltpu.roll(total, 64, 1)


def layer_kernel(sizes, *refs):
    ngx, ngy, ngz = sizes
    refs = list(refs)
    take = lambda n: [refs.pop(0) for _ in range(n)]
    feat_hbm, cot_hbm, skip_ref, bias_ref, modes_ref, in_ref, out_ref = take(7)
    hbm = dict(zip(NAMES, take(len(NAMES))))
    result_hbm, red_ref = take(2)
    tab = dict(zip(NAMES, take(len(NAMES))))
    (feat, cot, result, fs, half, quart, hs, qs, kh, kl, pr, rh, rl, qh, ql, th, tl, bs, t12, pre, gs, gqh, gql, ghh, ghl,
     wide, down, g12h, g12l, um, m2r, m0t, m1t, inw, outw, outt, skw, biast, gskip, gbias, pay, ra, rb, acc, red) = take(45)
    table_sem, local_sem, halo_send, halo_recv, red_send, red_recv = take(6)

    gx, gy, gz = lax.axis_index("gx"), lax.axis_index("gy"), lax.axis_index("gz")
    me = gx * ngz + gz
    group = ngx * ngz

    load_f = pltpu.make_async_copy(feat_hbm, feat, local_sem.at[0])
    load_f.start()
    load_c = pltpu.make_async_copy(cot_hbm, cot, local_sem.at[1])
    loads = {}
    for k, name in enumerate(NAMES):
        rows = table_shape(name)[0]
        src = hbm[name].at[pl.ds(pl.multiple_of(gz * rows, 16), rows)] if name in ("z1", "z2") else hbm[name]
        loads[name] = pltpu.make_async_copy(src, tab[name], table_sem.at[k])
        if k < 3:
            loads[name].start()

    barrier = pltpu.get_barrier_semaphore()

    def greet_row(k, carry):
        pl.semaphore_signal(
            barrier, inc=1, device_id=(gx, lax.rem(gy + k, ngy), gz), device_id_type=MESH
        )
        return carry

    lax.fori_loop(1, ngy, greet_row, 0)

    def greet_plane(k, carry):
        q = lax.rem(me + k, group)
        pl.semaphore_signal(
            barrier, inc=1, device_id=(q // ngz, gy, lax.rem(q, ngz)), device_id_type=MESH
        )
        return carry

    lax.fori_loop(1, group, greet_plane, 0)

    @pl.when(gx == 0)
    def _():
        for j in (1, 2):
            half[j, 0] = jnp.zeros((40, 640), F32)
        quart[1, 0] = jnp.zeros((40, 512), F32)

    @pl.when(gx == ngx - 1)
    def _():
        for j in (1, 2):
            half[j, 3] = jnp.zeros((40, 640), F32)
        quart[1, 2] = jnp.zeros((40, 512), F32)

    @pl.when(gy == 0)
    def _():
        for i in range(4):
            half[0, i] = jnp.zeros((40, 640), F32)
        for i in range(3):
            quart[0, i] = jnp.zeros((40, 512), F32)

    @pl.when(gy == ngy - 1)
    def _():
        for i in range(4):
            half[3, i] = jnp.zeros((40, 640), F32)
        for i in range(3):
            quart[2, i] = jnp.zeros((40, 512), F32)

    load_f.wait()
    for name in NAMES[3:]:
        loads[name].start()
        if name == "xy2":
            load_c.start()
    cells = feat[...].reshape(12, 2, 24, 768)
    hi, lo = split((cells[:, 0] + cells[:, 1]).reshape(288, 768))
    gs[0:288] = hi
    gs[288:576] = lo
    loads["pool"].wait()
    for n in range(3):
        pre[0:208, 256 * n : 256 * (n + 1)] = dot(tab["pool"][...], gs[0:576, 256 * n : 256 * (n + 1)])
    hi, lo = split(pre[0:208])
    loads["pair"].wait()
    for n in range(3):
        cols = slice(256 * n, 256 * (n + 1))
        cells = dot(lanes_cat(hi[0:160, cols], lo[0:160, cols]), tab["pair"][...])
        for j in range(2):
            for i in range(2):
                r = (j * 2 + i) * 40
                half[j + 1, i + 1, :, 128 * n : 128 * (n + 1)] = cells[r : r + 40]
    loads["quad"].wait()
    cells = dot(lanes_cat(hi[160:208], lo[160:208]), tab["quad"][...])
    quart[1, 1, :, 0:256] = cells[0:40]

    pl.semaphore_wait(barrier, ngy - 1 + group - 1)

    def remote(k, src, dst, to):
        return pltpu.make_async_remote_copy(
            src_ref=src,
            dst_ref=dst,
            send_sem=halo_send.at[k],
            recv_sem=halo_recv.at[k],
            device_id=to,
            device_id_type=MESH,
        )

    first = pl.multiple_of(128 * (1 - gz), 128)
    own, far = pl.ds(0, 384), pl.ds(384, 256)
    up_x, down_x = (gx + 1, gy, gz), (gx - 1, gy, gz)
    up_y, down_y = (gx, gy + 1, gz), (gx, gy - 1, gz)
    across = (gx, gy, 1 - gz)
    mid = pl.ds(1, 2)
    z_half = remote(0, half.at[mid, mid, :, pl.ds(first, 256)], half.at[mid, mid, :, far], across)
    z_quart = remote(1, quart.at[1, 1, :, pl.ds(0, 256)], quart.at[1, 1, :, pl.ds(256, 256)], across)
    x_up = [
        remote(2, half.at[mid, 2, :, own], half.at[mid, 0, :, own], up_x),
        remote(3, half.at[mid, 2, :, far], half.at[mid, 0, :, far], up_x),
        remote(4, quart.at[1, 1], quart.at[1, 0], up_x),
    ]
    x_down = [
        remote(5, half.at[mid, 1, :, own], half.at[mid, 3, :, own], down_x),
        remote(6, half.at[mid, 1, :, far], half.at[mid, 3, :, far], down_x),
        remote(7, quart.at[1, 1], quart.at[1, 2], down_x),
    ]
    y_up = [
        remote(8, half.at[2, mid, :, own], half.at[0, mid, :, own], up_y),
        remote(9, half.at[2, mid, :, far], half.at[0, mid, :, far], up_y),
        remote(10, half.at[2, 0], half.at[0, 0], up_y),
        remote(11, half.at[2, 3], half.at[0, 3], up_y),
        remote(12, quart.at[1], quart.at[0], up_y),
    ]
    y_down = [
        remote(13, half.at[1, mid, :, own], half.at[3, mid, :, own], down_y),
        remote(14, half.at[1, mid, :, far], half.at[3, mid, :, far], down_y),
        remote(15, half.at[1, 0], half.at[3, 0], down_y),
        remote(16, half.at[1, 3], half.at[3, 3], down_y),
        remote(17, quart.at[1], quart.at[2], down_y),
    ]

    def each(copies, which, to_up, to_down, act):
        @pl.when(to_up)
        def _():
            for k in which:
                act(copies[0][k])

        @pl.when(to_down)
        def _():
            for k in which:
                act(copies[1][k])

    has_ux, has_dx, has_uy, has_dy = gx < ngx - 1, gx > 0, gy < ngy - 1, gy > 0
    xs, ys = (x_up, x_down), (y_up, y_down)
    start = lambda c: c.start()
    recv = lambda c: c.wait_recv()
    sent = lambda c: c.wait_send()

    z_half.start()
    z_quart.start()
    each(xs, (0,), has_ux, has_dx, start)
    each(ys, (0,), has_uy, has_dy, start)

    def dup64(x):
        eye = (iota((64, 128), 0) == iota((64, 128), 1) % 64).astype(BF)
        return dot(x, eye)

    def dup32(x):
        eye = (iota((32, 128), 0) == iota((32, 128), 1) % 32).astype(BF)
        return dot(x, eye)

    diag_ir = iota((128, 256), 0) // 32 == iota((128, 256), 1) // 64
    diag_ro = iota((256, 128), 0) // 64 == iota((256, 128), 1) // 32
    diag_io = iota((128, 128), 0) // 32 == iota((128, 128), 1) // 32
    eye64 = (iota((64, 64), 0) == iota((64, 64), 1)).astype(BF)

    b0, b1 = split(jnp.broadcast_to(bias_ref[...], (16, 32)))
    biast[...] = (dup32(b0) + dup32(b1))[0:8]
    w0, w1 = [jnp.where(diag_io, rows_cat(*[dup32(w)] * 4), 0.0).astype(BF) for w in split(skip_ref[...])]
    w0 = lanes_cat(w0, w1)
    skw[...] = rows_cat(w0, w0)

    def spread(l, carry):
        i0, i1 = split(in_ref[l])
        o0, o1 = split(out_ref[l])

        def wide(w):
            t = dup64(w)
            return jnp.where(diag_ir, rows_cat(*[lanes_cat(t, t)] * 4), 0.0).astype(BF)

        def tall(w):
            t = dup32(dot(eye64, w, NT).astype(BF))
            return jnp.where(diag_ro, rows_cat(*[t] * 4), 0.0).astype(BF)

        w0 = wide(i0)
        inw[l] = rows_cat(w0, w0, wide(i1))
        w0 = wide(o0)
        outt[l] = rows_cat(w0, w0, wide(o1))
        w0 = lanes_cat(tall(o0), tall(o1))
        outw[l] = rows_cat(w0, w0)
        dup = []
        for d in range(3):
            m = modes_ref[l, d]
            hi, lo = split(m)
            rest = (m - hi.astype(F32) - lo.astype(F32)).astype(BF)
            dup.append(dup64(hi) + dup64(lo) + dup64(rest))
        m0t[l] = dup[0]
        m1t[l] = dup[1]
        um[l] = (dup[0][:, None, :] * dup[1][None, :, :]).reshape(256, 128)
        line = lanes_cat(*[dup[2]] * 8)
        line = jnp.where(iota((16, 1024), 0) == iota((16, 1024), 1) // 64, line, 0.0)
        m2r[l] = jnp.broadcast_to(jnp.sum(line, axis=0, keepdims=True), (8, 1024))
        return carry

    lax.fori_loop(0, 3, spread, 0)

    hi, lo = split(feat[...])
    fs[0:576] = hi
    fs[576:1152] = lo

    def stacked(ref):
        parts = [slice(128 * n, 128 * (n + 1)) for n in range(6)]
        return rows_cat(*[lanes_cat(ref[0:576, c], ref[576:1152, c]) for c in parts])

    def xy_transform(table, hi_lo, rows, chunks, wide):
        for n in range(chunks):
            cols = slice(wide * n, wide * (n + 1))
            data = rows_cat(hi_lo[0 : 2 * rows, cols], hi_lo[0:rows, cols])
            hi, lo = split(dot(table[...], data))
            th[:, cols] = hi
            tl[:, cols] = lo

    def z_transform(hi, lo, table, depth, into_h, into_l, l, parts=None):
        a = lanes_cat(hi, lo, hi)
        zh, zl = (0, depth) if parts is None else parts
        for n in range(2):
            cols = slice(256 * n, 256 * (n + 1))
            tz = rows_cat(table[zh : zh + depth, cols], table[zh : zh + depth, cols], table[zl : zl + depth, cols])
            vh, vl = split(dot(a, tz))
            into_h[l, :, cols] = vh
            into_l[l, :, cols] = vl

    quads = [(slice(128 * c, 128 * (c + 1)), slice(256 * c, 256 * (c + 1))) for c in range(4)]

    def modes_forward(l):
        data = [(kh[l, :, c], kl[l, :, c]) for c, _ in quads]
        p = dot(rows_cat(*[lanes_cat(a, b, a) for a, b in data]), inw[l])
        u = um[l]
        u = lanes_cat(u, u)
        data = []
        for k, (_, cols) in enumerate(quads):
            pk = p[256 * k : 256 * (k + 1)]
            pr[l, :, cols] = pk
            a, b = split(pk * u * m2r[l, 0:1, cols])
            rh[l, :, cols] = a
            rl[l, :, cols] = b
            data.append(lanes_cat(a, b))
        q = dot(rows_cat(*data), outw[l])
        q = q[:, 0:128] + q[:, 128:256]
        for k, (cols, _) in enumerate(quads):
            a, b = split(q[256 * k : 256 * (k + 1)])
            qh[l, :, cols] = a
            ql[l, :, cols] = b

    v = dot(stacked(fs), skw[...])
    v = v[:, 0:128] + v[:, 128:256] + biast[0:1]
    for n in range(6):
        pre[:, 128 * n : 128 * (n + 1)] = v[576 * n : 576 * (n + 1)]
    loads["xy0"].wait()
    xy_transform(tab["xy0"], fs, 576, 3, 256)

    z_half.wait_recv()
    z_quart.wait_recv()
    each(xs, (1, 2), has_ux, has_dx, start)
    each(ys, (1,), has_uy, has_dy, start)

    loads["z0"].wait()
    z_transform(th[...], tl[...], tab["z0"], 768, kh, kl, 0)
    modes_forward(0)

    each(xs, (0, 1, 2), has_dx, has_ux, recv)
    each(ys, (2, 3, 4), has_uy, has_dy, start)

    loads["z0t"].wait()
    a = lanes_cat(qh[0], ql[0], qh[0])
    for n in range(3):
        cols = slice(256 * n, 256 * (n + 1))
        tz = rows_cat(tab["z0t"][0:512, cols], tab["z0t"][0:512, cols], tab["z0t"][512:1024, cols])
        hi, lo = split(dot(a, tz))
        bs[0:256, cols] = hi
        bs[256:512, cols] = lo
    loads["inv"].wait()
    for n in range(3):
        cols = slice(256 * n, 256 * (n + 1))
        pre[:, cols] = pre[:, cols] + dot(tab["inv"][...], rows_cat(bs[0:512, cols], bs[0:256, cols]))

    each(ys, (0, 1, 2, 3, 4), has_dy, has_uy, recv)
    for j in range(4):
        hi, lo = split(half[j].reshape(160, 640))
        hs[160 * j : 160 * (j + 1)] = hi
        hs[640 + 160 * j : 640 + 160 * (j + 1)] = lo
    cells = rows_cat(quart[...].reshape(360, 512), jnp.zeros((8, 512), F32))
    hi, lo = split(cells)
    qs[0:368] = hi
    qs[368:736] = lo
    loads["xy1"].wait()
    xy_transform(tab["xy1"], hs, 640, 2, 256)
    data = rows_cat(hs[:, 512:640], hs[0:640, 512:640])
    hi, lo = split(dot(tab["xy1"][...], data))
    th[:, 512:640] = hi
    tl[:, 512:640] = lo
    loads["z1"].wait()
    z_transform(th[:, 0:640], tl[:, 0:640], tab["z1"], 640, kh, kl, 1)
    loads["xy2"].wait()
    xy_transform(tab["xy2"], qs, 368, 2, 256)
    loads["z2"].wait()
    z_transform(th[:, 0:512], tl[:, 0:512], tab["z2"], 512, kh, kl, 2)
    lax.fori_loop(1, 3, lambda l, c: (modes_forward(l), c)[1], 0)

    loads["z1c"].wait()
    loads["z2c"].wait()
    for l, name in ((1, "z1c"), (2, "z2c")):
        tz = tab[name]
        v = dot(lanes_cat(qh[l], ql[l], qh[l]), rows_cat(tz[0:512], tz[0:512], tz[512:1024]))
        hi, lo = split(v)
        t12[256 * (l - 1) : 256 * l] = hi
        t12[512 + 256 * (l - 1) : 512 + 256 * l] = lo
    loads["xy12"].wait()
    loads["unpair"].wait()
    s = dot(tab["xy12"][...], rows_cat(t12[...], t12[0:512]))
    for n in range(3):
        hi, lo = split(s[:, 128 * n : 128 * (n + 1)])
        v = dot(lanes_cat(hi, lo), tab["unpair"][...])
        for k in range(2):
            for step in range(2):
                wide[2 * n + k, pl.ds(step, 144, stride=2), :] = v[:, 128 * k : 128 * (k + 1)]

    load_c.wait()
    scale = 1.0 / math.sqrt(ngx * ngy * ngz * NP**3)
    c0 = math.sqrt(2.0 / math.pi)
    store = pltpu.make_async_copy(result, result_hbm, local_sem.at[2])

    def activate(m, carry):
        rows = pl.ds(pl.multiple_of(m * 48, 48), 48)
        v = lanes_cat(*[wide[n, pl.ds(pl.multiple_of(m * 24, 24), 24), :] for n in range(6)])
        x = pre[rows, :] + rows_cat(v, v)
        x2 = x * x
        t = jnp.tanh(c0 * (x * (1.0 + 0.044715 * x2)))
        half_t = 0.5 * (1.0 + t)
        result[rows, :] = x * half_t
        slope = half_t + 0.5 * x * (1.0 - t * t) * (c0 * (1.0 + (3 * 0.044715) * x2))
        g = cot[rows, :] * scale * slope
        hi, lo = split(g)
        gs[rows, :] = hi
        gs[pl.ds(pl.multiple_of(576 + m * 48, 48), 48), :] = lo
        g2 = g[0:24] + g[24:48]
        for n in range(6):
            down[n, pl.ds(pl.multiple_of(m * 24, 24), 24), :] = g2[:, 128 * n : 128 * (n + 1)]
        return carry + jnp.sum(g.reshape(6, 8, 768), axis=0)

    colsum = lax.fori_loop(0, 12, activate, jnp.zeros((8, 768), F32))
    store.start()
    gbias[...] = fold_lanes(colsum)

    xy_transform(tab["xy0"], gs, 576, 3, 256)
    z_transform(th[...], tl[...], tab["z0"], 768, gqh, gql, 0)
    for n in range(3):
        v = [down[2 * n + k, pl.ds(0, 144, stride=2), :] + down[2 * n + k, pl.ds(1, 144, stride=2), :] for k in range(2)]
        hi, lo = split(lanes_cat(*v))
        hi, lo = split(dot(lanes_cat(hi, lo), tab["pair"][...]))
        ghh[:, 128 * n : 128 * (n + 1)] = hi
        ghl[:, 128 * n : 128 * (n + 1)] = lo
    loads["xy12t"].wait()
    hi, lo = split(dot(tab["xy12t"][...], rows_cat(ghh[...], ghl[...], ghh[...])))
    g12h[...] = hi
    g12l[...] = lo
    loads["z2ct"].wait()
    z_transform(g12h[0:256], g12l[0:256], tab["z1"], 384, gqh, gql, 1, (0, 640))
    z_transform(g12h[256:512], g12l[256:512], tab["z2ct"], 384, gqh, gql, 2)

    total = dot(stacked(fs), stacked(gs), TN)
    total = total[0:128] + total[128:256]
    total = jnp.where(diag_io, total[:, 0:128] + total[:, 128:256], 0.0)
    s = total[0:32] + total[32:64] + total[64:96] + total[96:128]
    s = s + pltpu.roll(s, 64, 1)
    gskip[...] = s + pltpu.roll(s, 32, 1)

    def gram(ah, al, bh, bl):
        a, b = [], []
        for ca, cb in quads:
            x, y = ah[:, ca], al[:, ca]
            v, w = bh[:, cb], bl[:, cb]
            a += [x, y, x]
            b += [v, v, w]
        g = jnp.where(diag_ir, dot(rows_cat(*a), rows_cat(*b), TN), 0.0)
        return fold_lanes(g[0:32] + g[32:64] + g[64:96] + g[96:128])

    low = iota((32, 128), 1) < 64

    def modes_backward(l, carry):
        u = um[l]
        u = lanes_cat(u, u)
        e = jnp.zeros((256, 128), F32)
        g2 = []
        g_out = gram(gqh.at[l], gql.at[l], rh.at[l], rl.at[l])
        data = [(gqh[l, :, c], gql[l, :, c]) for c, _ in quads]
        g = dot(rows_cat(*[lanes_cat(a, b, a) for a, b in data]), outt[l])
        for k, (_, cols) in enumerate(quads):
            gr = g[256 * k : 256 * (k + 1)]
            d = gr * pr[l, :, cols]
            m2 = m2r[l, 0:1, cols]
            dm = d * m2
            e = e + dm[:, 0:128] + dm[:, 128:256]
            g2.append(jnp.sum((d * u).reshape(32, 8, 256), axis=0))
            hi, lo = split(gr * (u * m2))
            rh[l, :, cols] = hi
            rl[l, :, cols] = lo
        g_in = gram(kh.at[l], kl.at[l], rh.at[l], rl.at[l])
        e = (e + pltpu.roll(e, 64, 1)).reshape(16, 16, 128)
        g0 = jnp.sum(e * m1t[l][None, :, :], axis=1)
        g1 = jnp.sum(e * m0t[l][:, None, :], axis=0)
        g2 = jnp.sum(lanes_cat(*g2), axis=0, keepdims=True)
        g2 = jnp.where(iota((16, 1024), 0) == iota((16, 1024), 1) // 64, g2, 0.0)
        g2 = fold_lanes(g2)
        row = pl.multiple_of(l * 64, 64)
        pay[pl.ds(row, 32), :] = jnp.where(low, g_in, g_out)
        pay[pl.ds(row + 32, 16), :] = jnp.where(low[0:16], g0, g1)
        pay[pl.ds(row + 48, 16), :] = jnp.where(low[0:16], g2, 0.0)
        return carry

    lax.fori_loop(0, 3, modes_backward, 0)
    s = gskip[...]
    s = jnp.where(iota((16, 128), 1) < 96, s[0:16], s[16:32])
    pay[48:64] = jnp.where(low[0:16], pay[48:64], s)
    b = gbias[...] + pltpu.roll(gbias[...], 32, 1)
    b = jnp.broadcast_to(jnp.sum(b, axis=0, keepdims=True), (16, 128))
    pay[112:128] = jnp.where(low[0:16], pay[112:128], b)

    size = PAY // ngy

    def pushes(count, make, act):
        def body(k, carry):
            act(make(k))
            return carry

        lax.fori_loop(1, count, body, 0)

    def scatter(k):
        t = lax.rem(gy + k, ngy)
        return pltpu.make_async_remote_copy(
            src_ref=pay.at[pl.ds(pl.multiple_of(t * size, 8), size)],
            dst_ref=ra.at[k],
            send_sem=red_send.at[k],
            recv_sem=red_recv.at[k],
            device_id=(gx, t, gz),
            device_id_type=MESH,
        )

    def exchange(k):
        q = lax.rem(me + k, group)
        return pltpu.make_async_remote_copy(
            src_ref=acc,
            dst_ref=rb.at[me],
            send_sem=red_send.at[ngy + k],
            recv_sem=red_recv.at[ngy + k],
            device_id=(q // ngz, gy, lax.rem(q, ngz)),
            device_id_type=MESH,
        )

    mine = pl.ds(pl.multiple_of(gy * size, 8), size)

    def gather(k):
        t = lax.rem(gy + k, ngy)
        return pltpu.make_async_remote_copy(
            src_ref=red.at[mine],
            dst_ref=red.at[mine],
            send_sem=red_send.at[ngy + group + k],
            recv_sem=red_recv.at[ngy + group + k],
            device_id=(gx, t, gz),
            device_id_type=MESH,
        )

    pushes(ngy, scatter, start)
    pushes(ngy, scatter, recv)
    total = pay[mine]
    for k in range(1, ngy):
        total = total + ra[k]
    acc[...] = total
    rb[me] = total
    pushes(group, exchange, start)
    pushes(group, exchange, recv)
    total = rb[0]
    for k in range(1, group):
        total = total + rb[k]
    red[mine] = total
    pushes(ngy, gather, start)
    pushes(ngy, gather, recv)
    red_ref[...] = red[...]

    pushes(ngy, scatter, sent)
    pushes(group, exchange, sent)
    pushes(ngy, gather, sent)
    z_half.wait_send()
    z_quart.wait_send()
    each(xs, (0, 1, 2), has_ux, has_dx, sent)
    each(ys, (0, 1, 2, 3, 4), has_uy, has_dy, sent)
    store.wait()


def unpack_kernel(result_in, red, result_out, skip, bias, modes, fin, fout, held, sem):
    parts = [pl.ds(144 * k, 144) for k in range(4)]
    fetch = [pltpu.make_async_copy(result_in.at[p], held.at[p], sem.at[k]) for k, p in enumerate(parts)]
    store = [pltpu.make_async_copy(held.at[p], result_out.at[p], sem.at[4 + k]) for k, p in enumerate(parts)]
    for copy in fetch:
        copy.start()
    skip[0:16] = red[48:64, 64:96]
    skip[16:32] = red[48:64, 96:128]
    bias[...] = red[112:113, 64:96]
    for l in range(3):
        row = 64 * l
        fin[l] = red[row : row + 32, 0:64]
        fout[l] = red[row : row + 32, 64:128]
        modes[l, 0] = red[row + 32 : row + 48, 0:64]
        modes[l, 1] = red[row + 32 : row + 48, 64:128]
        modes[l, 2] = red[row + 48 : row + 64, 0:64]
    for a, b in zip(fetch, store):
        a.wait()
        b.start()
    for copy in store:
        copy.wait()


def solution(mesh):
    sizes = tuple(mesh.shape[name] for name in ("gx", "gy", "gz"))
    ngx, ngy, ngz = sizes
    group = ngx * ngz
    size = PAY // ngy
    any_spec = pl.BlockSpec(memory_space=pl.ANY)
    vmem_spec = pl.BlockSpec(memory_space=pltpu.VMEM)
    scratch = [pltpu.VMEM(table_shape(n), BF) for n in NAMES] + [
        pltpu.VMEM((576, 768), F32),
        pltpu.VMEM((576, 768), F32),
        pltpu.VMEM((576, 768), F32),
        pltpu.VMEM((1152, 768), BF),
        pltpu.VMEM((4, 4, 40, 640), F32),
        pltpu.VMEM((3, 3, 40, 512), F32),
        pltpu.VMEM((1280, 640), BF),
        pltpu.VMEM((736, 512), BF),
        pltpu.VMEM((3, 256, 512), BF),
        pltpu.VMEM((3, 256, 512), BF),
        pltpu.VMEM((3, 256, 1024), F32),
        pltpu.VMEM((3, 256, 1024), BF),
        pltpu.VMEM((3, 256, 1024), BF),
        pltpu.VMEM((3, 256, 512), BF),
        pltpu.VMEM((3, 256, 512), BF),
        pltpu.VMEM((256, 768), BF),
        pltpu.VMEM((256, 768), BF),
        pltpu.VMEM((512, 768), BF),
        pltpu.VMEM((1024, 384), BF),
        pltpu.VMEM((576, 768), F32),
        pltpu.VMEM((1152, 768), BF),
        pltpu.VMEM((3, 256, 512), BF),
        pltpu.VMEM((3, 256, 512), BF),
        pltpu.VMEM((144, 384), BF),
        pltpu.VMEM((144, 384), BF),
        pltpu.VMEM((6, 288, 128), F32),
        pltpu.VMEM((6, 288, 128), F32),
        pltpu.VMEM((512, 384), BF),
        pltpu.VMEM((512, 384), BF),
        pltpu.VMEM((3, 256, 128), F32),
        pltpu.VMEM((3, 8, 1024), F32),
        pltpu.VMEM((3, 16, 128), F32),
        pltpu.VMEM((3, 16, 128), F32),
        pltpu.VMEM((3, 384, 256), BF),
        pltpu.VMEM((3, 512, 256), BF),
        pltpu.VMEM((3, 384, 256), BF),
        pltpu.VMEM((256, 256), BF),
        pltpu.VMEM((8, 128), F32),
        pltpu.VMEM((32, 128), F32),
        pltpu.VMEM((8, 128), F32),
        pltpu.VMEM((PAY, 128), F32),
        pltpu.VMEM((ngy, size, 128), F32),
        pltpu.VMEM((group, size, 128), F32),
        pltpu.VMEM((size, 128), F32),
        pltpu.VMEM((PAY, 128), F32),
        pltpu.SemaphoreType.DMA((len(NAMES),)),
        pltpu.SemaphoreType.DMA((3,)),
        pltpu.SemaphoreType.DMA((18,)),
        pltpu.SemaphoreType.DMA((18,)),
        pltpu.SemaphoreType.DMA((2 * ngy + group,)),
        pltpu.SemaphoreType.DMA((2 * ngy + group,)),
    ]

    def per_device(features, cotangent, skip_weight, bias_vector, mode_factors, in_factors, out_factors):
        tables = [jnp.asarray(TABLES[n]) for n in NAMES]
        result, red = pl.pallas_call(
            lambda *refs: layer_kernel(sizes, *refs),
            name="layer",
            out_shape=(jax.ShapeDtypeStruct((576, 768), F32), jax.ShapeDtypeStruct((PAY, 128), F32)),
            in_specs=[any_spec] * 2 + [vmem_spec] * 5 + [any_spec] * len(NAMES),
            out_specs=(any_spec, vmem_spec),
            scratch_shapes=scratch,
            compiler_params=pltpu.CompilerParams(
                collective_id=0, has_side_effects=True, vmem_limit_bytes=60 * 1024 * 1024
            ),
            cost_estimate=pl.CostEstimate(flops=32 * 10**9, bytes_accessed=20 * 10**6, transcendentals=442368),
        )(
            features.reshape(576, 768),
            cotangent.reshape(576, 768),
            skip_weight,
            bias_vector.reshape(1, CH),
            mode_factors,
            in_factors,
            jnp.swapaxes(out_factors, 1, 2),
            *tables,
        )
        outs = pl.pallas_call(
            unpack_kernel,
            name="unpack",
            out_shape=(
                jax.ShapeDtypeStruct((576, 768), F32),
                jax.ShapeDtypeStruct((CH, CH), F32),
                jax.ShapeDtypeStruct((1, CH), F32),
                jax.ShapeDtypeStruct((3, 3, MD, RK), F32),
                jax.ShapeDtypeStruct((3, CH, RK), F32),
                jax.ShapeDtypeStruct((3, CH, RK), F32),
            ),
            in_specs=[any_spec, vmem_spec],
            out_specs=(any_spec,) + (vmem_spec,) * 5,
            scratch_shapes=[pltpu.VMEM((576, 768), F32), pltpu.SemaphoreType.DMA((8,))],
        )(result, red)
        return (outs[0].reshape(NP, NP, NP * CH), outs[1], outs[2].reshape(CH), outs[3], outs[4], jnp.swapaxes(outs[5], 1, 2))

    placed = (P("gx", "gy", "gz"), P("gx", "gy", "gz"), P(), P(), P(), P(), P())
    return jax.shard_map(
        per_device,
        mesh=mesh,
        in_specs=placed,
        out_specs=(P("gx", "gy", "gz"), P(), P(), P(), P(), P()),
        check_vma=False,
    )
```

time: 557 us -> 70.2 us (0.13); the launches traced: 549 us -> 69.9 us
  matrix products: 223 us -> 0 us
  waiting for transfers between devices: 170 us -> 0 us
  Pallas kernels: 0 us -> 69.1 us
  other arithmetic: 53 us -> 0 us
  local copies, waits for them, and re-layouts: 47.9 us -> 0 us
  starting transfers between devices: 39.9 us -> 0 us
  between operations: 15.5 us -> 0.8 us
    dot_general x44 -> x0, matrix products: 223 us -> none  [the longest x6 44 us: spectral(): return jnp.einsum('cz,xyco->xyzo', table, result, precision=HIGHEST)]
    psum x1 -> x0, waiting for transfers between devices: 144 us -> none  [per_device(): lax.psum((grads[0], grads[1], grads[2], grads[3], grads[4]), ('gx', 'gy',...]
    pallas_call x0 -> x2, Pallas kernels: none -> 69.1 us  [the longest x1 65.3 us: per_device(): pl.pallas_call(lambda *refs: layer_kernel(sizes, *refs), name='layer', ou...]
    reduce_sum x10 -> x0, other arithmetic: 40.5 us -> none  [the longest x2 21.9 us: upsample(): return jnp.repeat(block, factor, axis=2)]
    ppermute x12 -> x0, starting transfers between devices: 39.8 us -> none  [the longest x6 29 us: with_halo(): lax.ppermute(tail, axis, [(i, (i + 1) % count) for i in range(ends)])]
    ppermute x12 -> x0, waiting for transfers between devices: 26.6 us -> none  [the longest x6 23.3 us: with_halo(): lax.ppermute(head, axis, [((i + 1) % count, i) for i in range(ends)])]
    broadcast_in_dim x6 -> x0, local copies, waits for them, and re-layouts: 9.91 us -> none  [the longest x2 9.02 us: upsample(): return jnp.repeat(block, factor, axis=2)]
    reshape x2 -> x0, local copies, waits for them, and re-layouts: 9.73 us -> none  [the longest x1 5.61 us: per_device(): result.reshape(patch, patch, patch * channels)]
  transfers between devices with their start and end apart: 13 -> 0, of which waited for: 7 -> 0; matrix products, arithmetic and copies ran while one was open for 19% -> 0% of each run, Pallas kernels for 0% -> 0%
where the time goes in v1:
time: 70.2 us; the launch traced here: 69.9 us
  Pallas kernels  69.1 us (98%)
  between operations  0.8 us (1%)
    pallas_call x1, Pallas kernels, per_device(): pl.pallas_call(lambda *refs: layer_kernel(sizes, *refs), name='layer', ou...  65.3 us
    pallas_call x1, Pallas kernels, per_device(): pl.pallas_call(unpack_kernel, name='unpack', out_shape=(jax.ShapeDtypeStr...  3.85 us

profile of v1, /device:TPU:1, one launch (start us, length us, event | category | flops | bytes accessed | tf_op | source)
XLA Modules:
  0.0 69.9 jit_solution(2268456418175081750)
XLA Ops:
  0.6 65.3 %layer.1 = (f32[576,768]{1,0:T(8,128)}, f32[192,128]{1,0:T(8,128)}) custom-call(f32[576,768]{1,0:T(8,128)} %bitcast.7, f32[576,768]{1,0:T(8,128)} %bitcast.8, f32[32,32]{1,0:T(8,128)} %refs_2_.1, f32[1,32]{1,0:T(1,128)} %bitcast.12, f32[3,3,16,64]{3,2,1,0:T(8,128)} %refs_4_.1, f32[3,32,64]{2,1,0:T(8,128)} %refs_5_.1, f32[3,32,64]{2,1,0:T(8,128)} %bitcast.10, ...), custom_call_target="tpu_custom_call" | custom-call | flops 32000000000 | bytes 20000000 | tf_op jit(solution)/shard_map/layer/pallas_call | solution.py:759
  65.9 3.8 %unpack.1 = (f32[576,768]{1,0:T(8,128)}, f32[32,32]{1,0:T(8,128)}, f32[1,32]{1,0:T(1,128)}, f32[3,3,16,64]{3,2,1,0:T(8,128)}, f32[3,32,64]{2,1,0:T(8,128)}, /*index=5*/f32[3,32,64]{2,1,0:T(8,128)}) custom-call(f32[576,768]{1,0:T(8,128)} %get-tuple-element.14.result_in, f32[192,128]{1,0:T(8,128)} %get-tuple-element.15.red), custom_call_target="tpu_custom_call" | custom-call | tf_op jit(solution)/shard_map/unpack/pallas_call | solution.py:780

commit v2 on v0

v2 whole, which is shorter than its diff:
```python
import math

import jax
import jax.numpy as jnp
import ml_dtypes
import numpy as np
from jax import lax
from jax.experimental import pallas as pl
from jax.experimental.pallas import tpu as pltpu
from jax.sharding import PartitionSpec as P

MESH = pl.DeviceIdType.MESH
BF = jnp.bfloat16
F32 = jnp.float32
CH, RK, MD, NP = 32, 64, 16, 24
NN = (((1,), (0,)), ((), ()))
NT = (((1,), (1,)), ((), ()))
TN = (((0,), (0,)), ((), ()))
PAY = 192


def basis(length):
    rows = np.arange(MD)
    freq = np.where(rows < MD // 2, rows, rows - MD // 2 + 1).astype(np.float64)
    phase = 2.0 * math.pi / length * freq[:, None] * np.arange(length)[None, :]
    wave = np.where((rows < MD // 2)[:, None], np.cos(phase), np.sin(phase))
    return wave * math.sqrt(2.0 / length)


def halves(x):
    x = np.asarray(x, np.float32)
    hi = x.astype(ml_dtypes.bfloat16)
    lo = (x - hi.astype(np.float32)).astype(ml_dtypes.bfloat16)
    return hi, lo


def left(x):
    hi, lo = halves(x)
    return np.concatenate([hi, hi, lo], axis=1)


def right(x):
    hi, lo = halves(x)
    return np.concatenate([hi, lo], axis=0)


def exact(x, times, axis):
    x = np.asarray(x, np.float32).astype(ml_dtypes.bfloat16)
    return np.concatenate([x] * times, axis=axis)


def channel_eye(b):
    return np.kron(b, np.eye(CH))


def make_tables():
    b24, b18 = basis(24), basis(18)
    pool = np.zeros((208, 12, 24))
    for j in range(2):
        for i in range(2):
            for r in range(36):
                x, y = i * 6 + r // 6, 2 * (j * 6 + r % 6)
                pool[(j * 2 + i) * 40 + r, x, y : y + 2] = 1 / 8
    for r in range(36):
        x, y = 2 * (r // 6), 4 * (r % 6)
        pool[160 + r, x : x + 2, y : y + 4] = 1 / 64
    pool = pool.reshape(208, 288)
    pair = channel_eye(np.kron(np.eye(4), np.ones((2, 1))))
    quad = np.zeros((24, 8))
    for z in range(24):
        quad[z, z // 4] = 1
    quad = channel_eye(quad)
    xy0 = np.kron(b24, b24)
    xy1 = np.zeros((256, 4, 4, 40))
    for j in range(4):
        for i in range(4):
            for r in range(36):
                xy1[:, j, i, r] = np.kron(b24[:, i * 6 + r // 6], b24[:, j * 6 + r % 6])
    xy2 = np.zeros((256, 368))
    for j in range(3):
        for i in range(3):
            for r in range(36):
                xy2[:, (j * 3 + i) * 40 + r] = np.kron(
                    b18[:, i * 6 + r // 6], b18[:, j * 6 + r % 6]
                )
    z0 = channel_eye(b24.T)
    z1s, z2s = [], []
    for gz in range(2):
        z1 = np.zeros((20, 16))
        z1[0:12] = b24[:, 6:18].T
        if gz == 0:
            z1[12:18] = b24[:, 18:24].T
        else:
            z1[14:20] = b24[:, 0:6].T
        z1s.append(right(channel_eye(z1)))
        z2 = np.zeros((16, 16))
        z2[0:6] = b18[:, 6:12].T
        z2[8:14] = b18[:, 12:18].T if gz == 0 else b18[:, 0:6].T
        z2s.append(right(channel_eye(z2)))
    z1c = channel_eye(b24[:, 6:18])
    z2c = channel_eye(np.repeat(b18[:, 6:12], 2, axis=1))
    c1 = b24[:, 6:18]
    c2 = np.repeat(b18[:, 6:12], 2, axis=1)
    xy12 = np.concatenate([np.kron(c1, c1), np.kron(c2, c2)], axis=0)
    return {
        "pool": exact(pool, 2, 1),
        "pair": exact(pair, 2, 0),
        "quad": exact(quad, 2, 0),
        "unpair": exact(pair.T, 2, 0),
        "xy0": left(xy0),
        "z0": right(z0),
        "z0t": right(z0.T),
        "inv": left(xy0.T),
        "xy1": left(xy1.reshape(256, 640)),
        "z1": np.concatenate(z1s, axis=0),
        "xy2": left(xy2),
        "z2": np.concatenate(z2s, axis=0),
        "z1c": right(z1c),
        "z2c": right(z2c),
        "xy12": left(xy12.T),
        "xy12t": left(xy12),
        "z2ct": right(z2c.T),
    }


TABLES = make_tables()
NAMES = list(TABLES)


FED = ("hs", "qs", "pre", "fs", "kh0", "kl0", "pr0", "rh0", "rl0")
SHAPES = {
    "feat": ((576, 768), F32),
    "cot": ((576, 768), F32),
    "result": ((576, 768), F32),
    "fs": ((1152, 768), BF),
    "half": ((4, 4, 40, 640), F32),
    "quart": ((3, 3, 40, 512), F32),
    "hs": ((1280, 640), BF),
    "qs": ((736, 512), BF),
    "kh": ((3, 256, 512), BF),
    "kl": ((3, 256, 512), BF),
    "pr": ((3, 256, 1024), F32),
    "rh": ((3, 256, 1024), BF),
    "rl": ((3, 256, 1024), BF),
    "qh": ((3, 256, 512), BF),
    "ql": ((3, 256, 512), BF),
    "th": ((256, 768), BF),
    "tl": ((256, 768), BF),
    "bs": ((512, 768), BF),
    "t12": ((1024, 384), BF),
    "pre": ((576, 768), F32),
    "gs": ((1152, 768), BF),
    "gqh": ((3, 256, 512), BF),
    "gql": ((3, 256, 512), BF),
    "ghh": ((144, 384), BF),
    "ghl": ((144, 384), BF),
    "wide": ((6, 288, 128), F32),
    "down": ((6, 288, 128), F32),
    "g12h": ((512, 384), BF),
    "g12l": ((512, 384), BF),
    "um": ((3, 256, 128), F32),
    "m2r": ((3, 8, 1024), F32),
    "m0t": ((3, 16, 128), F32),
    "m1t": ((3, 16, 128), F32),
    "inw": ((3, 384, 256), BF),
    "outw": ((3, 512, 256), BF),
    "outt": ((3, 384, 256), BF),
    "skw": ((256, 256), BF),
    "biast": ((8, 128), F32),
    "gskip": ((32, 128), F32),
    "gbias": ((8, 128), F32),
    "pay": ((PAY, 128), F32),
    "red": ((PAY, 128), F32),
    "pooled": ((576, 768), BF),
    "strips": ((208, 768), F32),
    "result_hbm": ((576, 768), F32),
    "red_ref": ((PAY, 128), F32),
}
WEIGHTS = ("skip_ref", "bias_ref", "modes_ref", "in_ref", "out_ref")
SPREAD = ("um", "m2r", "m0t", "m1t", "inw", "outw", "outt")
KERNELS = {
    "A": {
        "ins": ("feat_hbm",) + WEIGHTS,
        "tables": ("pool", "pair", "quad", "xy0", "z0", "z0t", "inv"),
        "outs": tuple(n.rstrip("0") for n in FED),
        "scratch": ("feat", "pooled", "strips", "half", "quart", "qh", "ql", "th", "tl", "bs", "skw", "biast") + SPREAD,
    },
    "B": {
        "ins": ("cot_hbm",) + WEIGHTS + tuple(n + "_hbm" for n in FED),
        "tables": ("xy1", "z1", "xy2", "z2", "z1c", "z2c", "xy12", "unpair", "xy0", "z0", "pair", "xy12t", "z2ct"),
        "outs": ("result_hbm", "pay"),
        "scratch": ("cot", "result", "hs", "qs", "pre", "fs", "kh", "kl", "pr", "rh", "rl", "qh", "ql", "th", "tl", "t12", "gs")
        + ("gqh", "gql", "ghh", "ghl", "wide", "down", "g12h", "g12l", "gskip", "gbias")
        + SPREAD,
    },
    "C": {"ins": ("pay",), "tables": (), "outs": ("red_ref",), "scratch": ("ra", "rb", "acc", "red")},
}


def table_shape(name):
    rows, cols = TABLES[name].shape
    return (rows // 2 if name in ("z1", "z2") else rows), cols


def dot(a, b, dims=NN):
    return lax.dot_general(a, b, dims, preferred_element_type=F32)


def split(x):
    hi = x.astype(BF)
    return hi, (x - hi.astype(F32)).astype(BF)


def rows_cat(*parts):
    return jnp.concatenate(parts, axis=0)


def lanes_cat(*parts):
    return jnp.concatenate(parts, axis=1)


def iota(shape, dim):
    return lax.broadcasted_iota(jnp.int32, shape, dim)


def fold_lanes(x):
    total = x[:, 0:128]
    for k in range(1, x.shape[1] // 128):
        total = total + x[:, 128 * k : 128 * (k + 1)]
    return total + pltpu.roll(total, 64, 1)


def layer_kernel(sizes, parts, *refs):
    ngx, ngy, ngz = sizes
    names = KERNELS[parts]
    refs = list(refs)
    take = lambda which: dict(zip(which, [refs.pop(0) for _ in which]))
    used = names["tables"]
    R = take(names["ins"])
    hbm = take(used)
    R.update(take(names["outs"]))
    tab = take(used)
    R.update(take(names["scratch"]))
    table_sem, local_sem, halo_send, halo_recv, red_send, red_recv = refs

    gx, gy, gz = lax.axis_index("gx"), lax.axis_index("gy"), lax.axis_index("gz")
    me = gx * ngz + gz
    group = ngx * ngz

    loads = {}
    for k, name in enumerate(used):
        rows = table_shape(name)[0]
        src = hbm[name].at[pl.ds(pl.multiple_of(gz * rows, 16), rows)] if name in ("z1", "z2") else hbm[name]
        loads[name] = pltpu.make_async_copy(src, tab[name], table_sem.at[k])
    local = lambda k, src, dst: pltpu.make_async_copy(src, dst, local_sem.at[k])
    start = lambda c: c.start()
    recv = lambda c: c.wait_recv()
    sent = lambda c: c.wait_send()

    feat, fs, kh, kl, pr, rh, rl, qh = (R.get(n) for n in ("feat", "fs", "kh", "kl", "pr", "rh", "rl", "qh"))
    ql, th, tl, wide, um, m2r, m0t, m1t = (R.get(n) for n in ("ql", "th", "tl", "wide", "um", "m2r", "m0t", "m1t"))
    inw, outw, outt, skw, biast, skip_ref, bias_ref, modes_ref = (R.get(n) for n in ("inw", "outw", "outt", "skw", "biast", "skip_ref", "bias_ref", "modes_ref"))
    in_ref, out_ref = (R.get(n) for n in ("in_ref", "out_ref"))
    barrier = pltpu.get_barrier_semaphore() if parts != "B" else None

    def greet():
        def greet_row(k, carry):
            pl.semaphore_signal(
                barrier, inc=1, device_id=(gx, lax.rem(gy + k, ngy), gz), device_id_type=MESH
            )
            return carry

        lax.fori_loop(1, ngy, greet_row, 0)

        def greet_plane(k, carry):
            q = lax.rem(me + k, group)
            pl.semaphore_signal(
                barrier, inc=1, device_id=(q // ngz, gy, lax.rem(q, ngz)), device_id_type=MESH
            )
            return carry

        lax.fori_loop(1, group, greet_plane, 0)

    def dup64(x):
        eye = (iota((64, 128), 0) == iota((64, 128), 1) % 64).astype(BF)
        return dot(x, eye)

    def dup32(x):
        eye = (iota((32, 128), 0) == iota((32, 128), 1) % 32).astype(BF)
        return dot(x, eye)

    diag_ir = iota((128, 256), 0) // 32 == iota((128, 256), 1) // 64
    diag_ro = iota((256, 128), 0) // 64 == iota((256, 128), 1) // 32
    diag_io = iota((128, 128), 0) // 32 == iota((128, 128), 1) // 32
    eye64 = (iota((64, 64), 0) == iota((64, 64), 1)).astype(BF)

    def skip_weights():
        b0, b1 = split(jnp.broadcast_to(bias_ref[...], (16, 32)))
        biast[...] = (dup32(b0) + dup32(b1))[0:8]
        w0, w1 = [jnp.where(diag_io, rows_cat(*[dup32(w)] * 4), 0.0).astype(BF) for w in split(skip_ref[...])]
        w0 = lanes_cat(w0, w1)
        skw[...] = rows_cat(w0, w0)

    def spread_weights():
        def spread(l, carry):
            i0, i1 = split(in_ref[l])
            o0, o1 = split(out_ref[l])

            def wide(w):
                t = dup64(w)
                return jnp.where(diag_ir, rows_cat(*[lanes_cat(t, t)] * 4), 0.0).astype(BF)

            def tall(w):
                t = dup32(dot(eye64, w, NT).astype(BF))
                return jnp.where(diag_ro, rows_cat(*[t] * 4), 0.0).astype(BF)

            w0 = wide(i0)
            inw[l] = rows_cat(w0, w0, wide(i1))
            w0 = wide(o0)
            outt[l] = rows_cat(w0, w0, wide(o1))
            w0 = lanes_cat(tall(o0), tall(o1))
            outw[l] = rows_cat(w0, w0)
            dup = []
            for d in range(3):
                m = modes_ref[l, d]
                hi, lo = split(m)
                rest = (m - hi.astype(F32) - lo.astype(F32)).astype(BF)
                dup.append(dup64(hi) + dup64(lo) + dup64(rest))
            m0t[l] = dup[0]
            m1t[l] = dup[1]
            um[l] = (dup[0][:, None, :] * dup[1][None, :, :]).reshape(256, 128)
            line = lanes_cat(*[dup[2]] * 8)
            line = jnp.where(iota((16, 1024), 0) == iota((16, 1024), 1) // 64, line, 0.0)
            m2r[l] = jnp.broadcast_to(jnp.sum(line, axis=0, keepdims=True), (8, 1024))
            return carry

        lax.fori_loop(0, 3, spread, 0)

    def stacked(ref):
        parts = [slice(128 * n, 128 * (n + 1)) for n in range(6)]
        return rows_cat(*[lanes_cat(ref[0:576, c], ref[576:1152, c]) for c in parts])

    def xy_transform(table, hi_lo, rows, chunks, wide):
        for n in range(chunks):
            cols = slice(wide * n, wide * (n + 1))
            data = rows_cat(hi_lo[0 : 2 * rows, cols], hi_lo[0:rows, cols])
            hi, lo = split(dot(table[...], data))
            th[:, cols] = hi
            tl[:, cols] = lo

    def z_transform(hi, lo, table, depth, into_h, into_l, l, parts=None):
        a = lanes_cat(hi, lo, hi)
        zh, zl = (0, depth) if parts is None else parts
        for n in range(2):
            cols = slice(256 * n, 256 * (n + 1))
            tz = rows_cat(table[zh : zh + depth, cols], table[zh : zh + depth, cols], table[zl : zl + depth, cols])
            vh, vl = split(dot(a, tz))
            into_h[l, :, cols] = vh
            into_l[l, :, cols] = vl

    quads = [(slice(128 * c, 128 * (c + 1)), slice(256 * c, 256 * (c + 1))) for c in range(4)]

    def modes_forward(l):
        data = [(kh[l, :, c], kl[l, :, c]) for c, _ in quads]
        p = dot(rows_cat(*[lanes_cat(a, b, a) for a, b in data]), inw[l])
        u = um[l]
        u = lanes_cat(u, u)
        data = []
        for k, (_, cols) in enumerate(quads):
            pk = p[256 * k : 256 * (k + 1)]
            pr[l, :, cols] = pk
            a, b = split(pk * u * m2r[l, 0:1, cols])
            rh[l, :, cols] = a
            rl[l, :, cols] = b
            data.append(lanes_cat(a, b))
        q = dot(rows_cat(*data), outw[l])
        q = q[:, 0:128] + q[:, 128:256]
        for k, (cols, _) in enumerate(quads):
            a, b = split(q[256 * k : 256 * (k + 1)])
            qh[l, :, cols] = a
            ql[l, :, cols] = b

    def fine_part():
        feat, fs, half, quart, hs, qs, kh, kl = (R.get(n) for n in ("feat", "fs", "half", "quart", "hs", "qs", "kh", "kl"))
        qh, ql, th, tl, bs, pre, skw, biast = (R.get(n) for n in ("qh", "ql", "th", "tl", "bs", "pre", "skw", "biast"))
        pooled, strips = (R.get(n) for n in ("pooled", "strips"))
        load_f = local(0, R["feat_hbm"], feat)
        load_f.start()
        for name in used[:3]:
            loads[name].start()
        greet()
        @pl.when(gx == 0)
        def _():
            for j in (1, 2):
                half[j, 0] = jnp.zeros((40, 640), F32)
            quart[1, 0] = jnp.zeros((40, 512), F32)

        @pl.when(gx == ngx - 1)
        def _():
            for j in (1, 2):
                half[j, 3] = jnp.zeros((40, 640), F32)
            quart[1, 2] = jnp.zeros((40, 512), F32)

        @pl.when(gy == 0)
        def _():
            for i in range(4):
                half[0, i] = jnp.zeros((40, 640), F32)
            for i in range(3):
                quart[0, i] = jnp.zeros((40, 512), F32)

        @pl.when(gy == ngy - 1)
        def _():
            for i in range(4):
                half[3, i] = jnp.zeros((40, 640), F32)
            for i in range(3):
                quart[2, i] = jnp.zeros((40, 512), F32)

        load_f.wait()
        for name in used[3:]:
            loads[name].start()
        cells = feat[...].reshape(12, 2, 24, 768)
        hi, lo = split((cells[:, 0] + cells[:, 1]).reshape(288, 768))
        pooled[0:288] = hi
        pooled[288:576] = lo
        loads["pool"].wait()
        for n in range(3):
            strips[:, 256 * n : 256 * (n + 1)] = dot(tab["pool"][...], pooled[:, 256 * n : 256 * (n + 1)])
        hi, lo = split(strips[...])
        loads["pair"].wait()
        for n in range(3):
            cols = slice(256 * n, 256 * (n + 1))
            cells = dot(lanes_cat(hi[0:160, cols], lo[0:160, cols]), tab["pair"][...])
            for j in range(2):
                for i in range(2):
                    r = (j * 2 + i) * 40
                    half[j + 1, i + 1, :, 128 * n : 128 * (n + 1)] = cells[r : r + 40]
        loads["quad"].wait()
        cells = dot(lanes_cat(hi[160:208], lo[160:208]), tab["quad"][...])
        quart[1, 1, :, 0:256] = cells[0:40]

        pl.semaphore_wait(barrier, ngy - 1 + group - 1)

        def remote(k, src, dst, to):
            return pltpu.make_async_remote_copy(
                src_ref=src,
                dst_ref=dst,
                send_sem=halo_send.at[k],
                recv_sem=halo_recv.at[k],
                device_id=to,
                device_id_type=MESH,
            )

        first = pl.multiple_of(128 * (1 - gz), 128)
        own, far = pl.ds(0, 384), pl.ds(384, 256)
        up_x, down_x = (gx + 1, gy, gz), (gx - 1, gy, gz)
        up_y, down_y = (gx, gy + 1, gz), (gx, gy - 1, gz)
        across = (gx, gy, 1 - gz)
        mid = pl.ds(1, 2)
        z_half = remote(0, half.at[mid, mid, :, pl.ds(first, 256)], half.at[mid, mid, :, far], across)
        z_quart = remote(1, quart.at[1, 1, :, pl.ds(0, 256)], quart.at[1, 1, :, pl.ds(256, 256)], across)
        x_up = [
            remote(2, half.at[mid, 2, :, own], half.at[mid, 0, :, own], up_x),
            remote(3, half.at[mid, 2, :, far], half.at[mid, 0, :, far], up_x),
            remote(4, quart.at[1, 1], quart.at[1, 0], up_x),
        ]
        x_down = [
            remote(5, half.at[mid, 1, :, own], half.at[mid, 3, :, own], down_x),
            remote(6, half.at[mid, 1, :, far], half.at[mid, 3, :, far], down_x),
            remote(7, quart.at[1, 1], quart.at[1, 2], down_x),
        ]
        y_up = [
            remote(8, half.at[2, mid, :, own], half.at[0, mid, :, own], up_y),
            remote(9, half.at[2, mid, :, far], half.at[0, mid, :, far], up_y),
            remote(10, half.at[2, 0], half.at[0, 0], up_y),
            remote(11, half.at[2, 3], half.at[0, 3], up_y),
            remote(12, quart.at[1], quart.at[0], up_y),
        ]
        y_down = [
            remote(13, half.at[1, mid, :, own], half.at[3, mid, :, own], down_y),
            remote(14, half.at[1, mid, :, far], half.at[3, mid, :, far], down_y),
            remote(15, half.at[1, 0], half.at[3, 0], down_y),
            remote(16, half.at[1, 3], half.at[3, 3], down_y),
            remote(17, quart.at[1], quart.at[2], down_y),
        ]

        def each(copies, which, to_up, to_down, act):
            @pl.when(to_up)
            def _():
                for k in which:
                    act(copies[0][k])

            @pl.when(to_down)
            def _():
                for k in which:
                    act(copies[1][k])

        has_ux, has_dx, has_uy, has_dy = gx < ngx - 1, gx > 0, gy < ngy - 1, gy > 0
        xs, ys = (x_up, x_down), (y_up, y_down)

        z_half.start()
        z_quart.start()
        each(xs, (0,), has_ux, has_dx, start)
        each(ys, (0,), has_uy, has_dy, start)

        skip_weights()
        spread_weights()
        hi, lo = split(feat[...])
        fs[0:576] = hi
        fs[576:1152] = lo

        v = dot(stacked(fs), skw[...])
        v = v[:, 0:128] + v[:, 128:256] + biast[0:1]
        for n in range(6):
            pre[:, 128 * n : 128 * (n + 1)] = v[576 * n : 576 * (n + 1)]
        loads["xy0"].wait()
        xy_transform(tab["xy0"], fs, 576, 3, 256)

        z_half.wait_recv()
        z_quart.wait_recv()
        each(xs, (1, 2), has_ux, has_dx, start)
        each(ys, (1,), has_uy, has_dy, start)

        loads["z0"].wait()
        z_transform(th[...], tl[...], tab["z0"], 768, kh, kl, 0)
        modes_forward(0)

        each(xs, (0, 1, 2), has_dx, has_ux, recv)
        each(ys, (2, 3, 4), has_uy, has_dy, start)

        loads["z0t"].wait()
        a = lanes_cat(qh[0], ql[0], qh[0])
        for n in range(3):
            cols = slice(256 * n, 256 * (n + 1))
            tz = rows_cat(tab["z0t"][0:512, cols], tab["z0t"][0:512, cols], tab["z0t"][512:1024, cols])
            hi, lo = split(dot(a, tz))
            bs[0:256, cols] = hi
            bs[256:512, cols] = lo
        loads["inv"].wait()
        for n in range(3):
            cols = slice(256 * n, 256 * (n + 1))
            pre[:, cols] = pre[:, cols] + dot(tab["inv"][...], rows_cat(bs[0:512, cols], bs[0:256, cols]))

        each(ys, (0, 1, 2, 3, 4), has_dy, has_uy, recv)
        for j in range(4):
            hi, lo = split(half[j].reshape(160, 640))
            hs[160 * j : 160 * (j + 1)] = hi
            hs[640 + 160 * j : 640 + 160 * (j + 1)] = lo
        cells = rows_cat(quart[...].reshape(360, 512), jnp.zeros((8, 512), F32))
        hi, lo = split(cells)
        qs[0:368] = hi
        qs[368:736] = lo
        z_half.wait_send()
        z_quart.wait_send()
        each(xs, (0, 1, 2), has_ux, has_dx, sent)
        each(ys, (0, 1, 2, 3, 4), has_uy, has_dy, sent)

    def coarse_part():
        cot, result, fs, half, hs, qs, kh, kl = (R.get(n) for n in ("cot", "result", "fs", "half", "hs", "qs", "kh", "kl"))
        pr, rh, rl, qh, ql, th, tl, t12 = (R.get(n) for n in ("pr", "rh", "rl", "qh", "ql", "th", "tl", "t12"))
        pre, gs, gqh, gql, ghh, ghl, wide, down = (R.get(n) for n in ("pre", "gs", "gqh", "gql", "ghh", "ghl", "wide", "down"))
        g12h, g12l, um, m2r, m0t, m1t, outt, gskip = (R.get(n) for n in ("g12h", "g12l", "um", "m2r", "m0t", "m1t", "outt", "gskip"))
        gbias, pay, result_hbm = (R.get(n) for n in ("gbias", "pay", "result_hbm"))
        got = {}
        for k, name in enumerate(FED):
            src, dst = R[name + "_hbm"], R[name.rstrip("0")]
            got[name] = local(2 + k, src.at[0], dst.at[0]) if name.endswith("0") else local(2 + k, src, dst)
        load_c = local(0, R["cot_hbm"], cot)
        for name in ("hs", "qs"):
            got[name].start()
        for name in used:
            loads[name].start()
            if name == "xy2":
                load_c.start()
                for name in FED:
                    if name not in ("hs", "qs"):
                        got[name].start()
        spread_weights()
        got["hs"].wait()
        got["qs"].wait()
        loads["xy1"].wait()
        xy_transform(tab["xy1"], hs, 640, 2, 256)
        data = rows_cat(hs[:, 512:640], hs[0:640, 512:640])
        hi, lo = split(dot(tab["xy1"][...], data))
        th[:, 512:640] = hi
        tl[:, 512:640] = lo
        loads["z1"].wait()
        z_transform(th[:, 0:640], tl[:, 0:640], tab["z1"], 640, kh, kl, 1)
        loads["xy2"].wait()
        xy_transform(tab["xy2"], qs, 368, 2, 256)
        loads["z2"].wait()
        z_transform(th[:, 0:512], tl[:, 0:512], tab["z2"], 512, kh, kl, 2)
        lax.fori_loop(1, 3, lambda l, c: (modes_forward(l), c)[1], 0)

        loads["z1c"].wait()
        loads["z2c"].wait()
        for l, name in ((1, "z1c"), (2, "z2c")):
            tz = tab[name]
            v = dot(lanes_cat(qh[l], ql[l], qh[l]), rows_cat(tz[0:512], tz[0:512], tz[512:1024]))
            hi, lo = split(v)
            t12[256 * (l - 1) : 256 * l] = hi
            t12[512 + 256 * (l - 1) : 512 + 256 * l] = lo
        loads["xy12"].wait()
        loads["unpair"].wait()
        s = dot(tab["xy12"][...], rows_cat(t12[...], t12[0:512]))
        for n in range(3):
            hi, lo = split(s[:, 128 * n : 128 * (n + 1)])
            v = dot(lanes_cat(hi, lo), tab["unpair"][...])
            for k in range(2):
                for step in range(2):
                    wide[2 * n + k, pl.ds(step, 144, stride=2), :] = v[:, 128 * k : 128 * (k + 1)]

        load_c.wait()
        got["pre"].wait()
        scale = 1.0 / math.sqrt(ngx * ngy * ngz * NP**3)
        c0 = math.sqrt(2.0 / math.pi)

        def activate(m, carry):
            rows = pl.ds(pl.multiple_of(m * 48, 48), 48)
            v = lanes_cat(*[wide[n, pl.ds(pl.multiple_of(m * 24, 24), 24), :] for n in range(6)])
            x = pre[rows, :] + rows_cat(v, v)
            x2 = x * x
            t = jnp.tanh(c0 * (x * (1.0 + 0.044715 * x2)))
            half_t = 0.5 * (1.0 + t)
            result[rows, :] = x * half_t
            slope = half_t + 0.5 * x * (1.0 - t * t) * (c0 * (1.0 + (3 * 0.044715) * x2))
            g = cot[rows, :] * scale * slope
            hi, lo = split(g)
            gs[rows, :] = hi
            gs[pl.ds(pl.multiple_of(576 + m * 48, 48), 48), :] = lo
            g2 = g[0:24] + g[24:48]
            for n in range(6):
                down[n, pl.ds(pl.multiple_of(m * 24, 24), 24), :] = g2[:, 128 * n : 128 * (n + 1)]
            return carry + jnp.sum(g.reshape(6, 8, 768), axis=0)

        colsum = lax.fori_loop(0, 12, activate, jnp.zeros((8, 768), F32))
        store = local(1, result, result_hbm)
        store.start()
        gbias[...] = fold_lanes(colsum)

        for name in ("xy0", "z0", "pair"):
            loads[name].wait()
        xy_transform(tab["xy0"], gs, 576, 3, 256)
        z_transform(th[...], tl[...], tab["z0"], 768, gqh, gql, 0)
        for n in range(3):
            v = [down[2 * n + k, pl.ds(0, 144, stride=2), :] + down[2 * n + k, pl.ds(1, 144, stride=2), :] for k in range(2)]
            hi, lo = split(lanes_cat(*v))
            hi, lo = split(dot(lanes_cat(hi, lo), tab["pair"][...]))
            ghh[:, 128 * n : 128 * (n + 1)] = hi
            ghl[:, 128 * n : 128 * (n + 1)] = lo
        loads["xy12t"].wait()
        hi, lo = split(dot(tab["xy12t"][...], rows_cat(ghh[...], ghl[...], ghh[...])))
        g12h[...] = hi
        g12l[...] = lo
        loads["z2ct"].wait()
        z_transform(g12h[0:256], g12l[0:256], tab["z1"], 384, gqh, gql, 1, (0, 640))
        z_transform(g12h[256:512], g12l[256:512], tab["z2ct"], 384, gqh, gql, 2)

        for name in ("fs", "kh0", "kl0", "pr0", "rh0", "rl0"):
            got[name].wait()
        total = dot(stacked(fs), stacked(gs), TN)
        total = total[0:128] + total[128:256]
        total = jnp.where(diag_io, total[:, 0:128] + total[:, 128:256], 0.0)
        s = total[0:32] + total[32:64] + total[64:96] + total[96:128]
        s = s + pltpu.roll(s, 64, 1)
        gskip[...] = s + pltpu.roll(s, 32, 1)

        def gram(ah, al, bh, bl):
            a, b = [], []
            for ca, cb in quads:
                x, y = ah[:, ca], al[:, ca]
                v, w = bh[:, cb], bl[:, cb]
                a += [x, y, x]
                b += [v, v, w]
            g = jnp.where(diag_ir, dot(rows_cat(*a), rows_cat(*b), TN), 0.0)
            return fold_lanes(g[0:32] + g[32:64] + g[64:96] + g[96:128])

        low = iota((32, 128), 1) < 64

        def modes_backward(l, carry):
            u = um[l]
            u = lanes_cat(u, u)
            e = jnp.zeros((256, 128), F32)
            g2 = []
            g_out = gram(gqh.at[l], gql.at[l], rh.at[l], rl.at[l])
            data = [(gqh[l, :, c], gql[l, :, c]) for c, _ in quads]
            g = dot(rows_cat(*[lanes_cat(a, b, a) for a, b in data]), outt[l])
            for k, (_, cols) in enumerate(quads):
                gr = g[256 * k : 256 * (k + 1)]
                d = gr * pr[l, :, cols]
                m2 = m2r[l, 0:1, cols]
                dm = d * m2
                e = e + dm[:, 0:128] + dm[:, 128:256]
                g2.append(jnp.sum((d * u).reshape(32, 8, 256), axis=0))
                hi, lo = split(gr * (u * m2))
                rh[l, :, cols] = hi
                rl[l, :, cols] = lo
            g_in = gram(kh.at[l], kl.at[l], rh.at[l], rl.at[l])
            e = (e + pltpu.roll(e, 64, 1)).reshape(16, 16, 128)
            g0 = jnp.sum(e * m1t[l][None, :, :], axis=1)
            g1 = jnp.sum(e * m0t[l][:, None, :], axis=0)
            g2 = jnp.sum(lanes_cat(*g2), axis=0, keepdims=True)
            g2 = jnp.where(iota((16, 1024), 0) == iota((16, 1024), 1) // 64, g2, 0.0)
            g2 = fold_lanes(g2)
            row = pl.multiple_of(l * 64, 64)
            pay[pl.ds(row, 32), :] = jnp.where(low, g_in, g_out)
            pay[pl.ds(row + 32, 16), :] = jnp.where(low[0:16], g0, g1)
            pay[pl.ds(row + 48, 16), :] = jnp.where(low[0:16], g2, 0.0)
            return carry

        lax.fori_loop(0, 3, modes_backward, 0)
        s = gskip[...]
        s = jnp.where(iota((16, 128), 1) < 96, s[0:16], s[16:32])
        pay[48:64] = jnp.where(low[0:16], pay[48:64], s)
        b = gbias[...] + pltpu.roll(gbias[...], 32, 1)
        b = jnp.broadcast_to(jnp.sum(b, axis=0, keepdims=True), (16, 128))
        pay[112:128] = jnp.where(low[0:16], pay[112:128], b)

        store.wait()

    def sum_part():
        pay, ra, rb, acc, red, red_ref = (R.get(n) for n in ("pay", "ra", "rb", "acc", "red", "red_ref"))
        greet()
        pl.semaphore_wait(barrier, ngy - 1 + group - 1)
        size = PAY // ngy

        def pushes(count, make, act):
            def body(k, carry):
                act(make(k))
                return carry

            lax.fori_loop(1, count, body, 0)

        def scatter(k):
            t = lax.rem(gy + k, ngy)
            return pltpu.make_async_remote_copy(
                src_ref=pay.at[pl.ds(pl.multiple_of(t * size, 8), size)],
                dst_ref=ra.at[k],
                send_sem=red_send.at[k],
                recv_sem=red_recv.at[k],
                device_id=(gx, t, gz),
                device_id_type=MESH,
            )

        def exchange(k):
            q = lax.rem(me + k, group)
            return pltpu.make_async_remote_copy(
                src_ref=acc,
                dst_ref=rb.at[me],
                send_sem=red_send.at[ngy + k],
                recv_sem=red_recv.at[ngy + k],
                device_id=(q // ngz, gy, lax.rem(q, ngz)),
                device_id_type=MESH,
            )

        mine = pl.ds(pl.multiple_of(gy * size, 8), size)

        def gather(k):
            t = lax.rem(gy + k, ngy)
            return pltpu.make_async_remote_copy(
                src_ref=red.at[mine],
                dst_ref=red.at[mine],
                send_sem=red_send.at[ngy + group + k],
                recv_sem=red_recv.at[ngy + group + k],
                device_id=(gx, t, gz),
                device_id_type=MESH,
            )

        pushes(ngy, scatter, start)
        pushes(ngy, scatter, recv)
        total = pay[mine]
        for k in range(1, ngy):
            total = total + ra[k]
        acc[...] = total
        rb[me] = total
        pushes(group, exchange, start)
        pushes(group, exchange, recv)
        total = rb[0]
        for k in range(1, group):
            total = total + rb[k]
        red[mine] = total
        pushes(ngy, gather, start)
        pushes(ngy, gather, recv)
        red_ref[...] = red[...]

        pushes(ngy, scatter, sent)
        pushes(group, exchange, sent)
        pushes(ngy, gather, sent)

    {"A": fine_part, "B": coarse_part, "C": sum_part}[parts]()


def unpack_kernel(red, skip, bias, modes, fin, fout):
    skip[0:16] = red[48:64, 64:96]
    skip[16:32] = red[48:64, 96:128]
    bias[...] = red[112:113, 64:96]
    for l in range(3):
        row = 64 * l
        fin[l] = red[row : row + 32, 0:64]
        fout[l] = red[row : row + 32, 64:128]
        modes[l, 0] = red[row + 32 : row + 48, 0:64]
        modes[l, 1] = red[row + 32 : row + 48, 64:128]
        modes[l, 2] = red[row + 48 : row + 64, 0:64]


def solution(mesh):
    sizes = tuple(mesh.shape[name] for name in ("gx", "gy", "gz"))
    ngx, ngy, ngz = sizes
    group = ngx * ngz
    size = PAY // ngy
    any_spec = pl.BlockSpec(memory_space=pl.ANY)
    vmem_spec = pl.BlockSpec(memory_space=pltpu.VMEM)
    shapes = dict(SHAPES)
    shapes.update(ra=((ngy, size, 128), F32), rb=((group, size, 128), F32), acc=((size, 128), F32))

    def call(part, args, flops):
        names = KERNELS[part]

        def out_shape(n):
            shape, kind = shapes[n]
            if part == "A" and len(shape) == 3:
                shape = (1,) + shape[1:]
            return jax.ShapeDtypeStruct(shape, kind)

        remote = {} if part == "B" else {"collective_id": "AC".index(part), "has_side_effects": True}
        return pl.pallas_call(
            lambda *refs: layer_kernel(sizes, part, *refs),
            name="part_" + part.lower(),
            out_shape=tuple(out_shape(n) for n in names["outs"]),
            in_specs=[any_spec if n.endswith("hbm") else vmem_spec for n in names["ins"]] + [any_spec] * len(names["tables"]),
            out_specs=tuple(any_spec if n.endswith("hbm") else vmem_spec for n in names["outs"]),
            scratch_shapes=[pltpu.VMEM(table_shape(n), BF) for n in names["tables"]]
            + [pltpu.VMEM(*shapes[n]) for n in names["scratch"]]
            + [
                pltpu.SemaphoreType.DMA((max(1, len(names["tables"])),)),
                pltpu.SemaphoreType.DMA((2 + len(FED),)),
                pltpu.SemaphoreType.DMA((18,)),
                pltpu.SemaphoreType.DMA((18,)),
                pltpu.SemaphoreType.DMA((2 * ngy + group,)),
                pltpu.SemaphoreType.DMA((2 * ngy + group,)),
            ],
            compiler_params=pltpu.CompilerParams(vmem_limit_bytes=58 * 1024 * 1024, **remote),
            cost_estimate=pl.CostEstimate(flops=flops, bytes_accessed=10 * 10**6, transcendentals=442368),
        )(*args, *[jnp.asarray(TABLES[n]) for n in names["tables"]])

    def per_device(features, cotangent, skip_weight, bias_vector, mode_factors, in_factors, out_factors):
        weights = (skip_weight, bias_vector.reshape(1, CH), mode_factors, in_factors, jnp.swapaxes(out_factors, 1, 2))
        fed = call("A", (features.reshape(576, 768), *weights), 5 * 10**9)
        result, pay = call("B", (cotangent.reshape(576, 768), *weights, *fed), 10**10)
        (red,) = call("C", (pay,), 10**6)
        outs = pl.pallas_call(
            unpack_kernel,
            name="unpack",
            out_shape=(
                jax.ShapeDtypeStruct((CH, CH), F32),
                jax.ShapeDtypeStruct((1, CH), F32),
                jax.ShapeDtypeStruct((3, 3, MD, RK), F32),
                jax.ShapeDtypeStruct((3, CH, RK), F32),
                jax.ShapeDtypeStruct((3, CH, RK), F32),
            ),
            in_specs=[vmem_spec],
            out_specs=(vmem_spec,) * 5,
        )(red)
        return (result.reshape(NP, NP, NP * CH), outs[0], outs[1].reshape(CH), outs[2], outs[3], jnp.swapaxes(outs[4], 1, 2))

    placed = (P("gx", "gy", "gz"), P("gx", "gy", "gz"), P(), P(), P(), P(), P())
    return jax.shard_map(
        per_device,
        mesh=mesh,
        in_specs=placed,
        out_specs=(P("gx", "gy", "gz"), P(), P(), P(), P(), P()),
        check_vma=False,
    )
```

time: 557 us -> 82 us (0.15); the launches traced: 549 us -> 81.7 us
  matrix products: 223 us -> 0 us
  waiting for transfers between devices: 170 us -> 0 us
  Pallas kernels: 0 us -> 81 us
  other arithmetic: 53 us -> 0 us
  local copies, waits for them, and re-layouts: 47.9 us -> 0 us
  starting transfers between devices: 39.9 us -> 0 us
  between operations: 15.5 us -> 0.66 us
    dot_general x44 -> x0, matrix products: 223 us -> none  [the longest x6 44 us: spectral(): return jnp.einsum('cz,xyco->xyzo', table, result, precision=HIGHEST)]
    psum x1 -> x0, waiting for transfers between devices: 144 us -> none  [per_device(): lax.psum((grads[0], grads[1], grads[2], grads[3], grads[4]), ('gx', 'gy',...]
    pallas_call x0 -> x4, Pallas kernels: none -> 81 us  [the longest x3 79.4 us: call(): pl.pallas_call(lambda *refs: layer_kernel(sizes, part, *refs), name='part...]
    reduce_sum x10 -> x0, other arithmetic: 40.5 us -> none  [the longest x2 21.9 us: upsample(): return jnp.repeat(block, factor, axis=2)]
    ppermute x12 -> x0, starting transfers between devices: 39.8 us -> none  [the longest x6 29 us: with_halo(): lax.ppermute(tail, axis, [(i, (i + 1) % count) for i in range(ends)])]
    ppermute x12 -> x0, waiting for transfers between devices: 26.6 us -> none  [the longest x6 23.3 us: with_halo(): lax.ppermute(head, axis, [((i + 1) % count, i) for i in range(ends)])]
    broadcast_in_dim x6 -> x0, local copies, waits for them, and re-layouts: 9.91 us -> none  [the longest x2 9.02 us: upsample(): return jnp.repeat(block, factor, axis=2)]
    reshape x2 -> x0, local copies, waits for them, and re-layouts: 9.73 us -> none  [the longest x1 5.61 us: per_device(): result.reshape(patch, patch, patch * channels)]
  transfers between devices with their start and end apart: 13 -> 0, of which waited for: 7 -> 0; matrix products, arithmetic and copies ran while one was open for 19% -> 0% of each run, Pallas kernels for 0% -> 0%
where the time goes in v2:
time: 82 us; the launch traced here: 81.7 us
  Pallas kernels  81 us (99%)
    pallas_call x3, Pallas kernels, call(): pl.pallas_call(lambda *refs: layer_kernel(sizes, part, *refs), name='part...  79.4 us

profile of v2, /device:TPU:1, one launch (start us, length us, event | category | flops | bytes accessed | tf_op | source)
XLA Modules:
  0.0 81.7 jit_solution(9015061837114658818)
XLA Ops:
  0.6 35.3 %part_a.1 = (bf16[1280,640]{1,0:T(8,128)(2,1)}, bf16[736,512]{1,0:T(8,128)(2,1)}, f32[576,768]{1,0:T(8,128)}, bf16[1152,768]{1,0:T(8,128)(2,1)}, bf16[1,256,512]...) custom-call(f32[576,768]{1,0:T(8,128)} %bitcast.7, ...), custom_call_target="tpu_custom_call" | custom-call | flops 5000000000 | bytes 10000000 | tf_op jit(solution)/shard_map/part_a/pallas_call | solution.py:825
  35.9 23.0 %part_b.1 = (f32[576,768]{1,0:T(8,128)}, f32[192,128]{1,0:T(8,128)}) custom-call(f32[576,768]{1,0:T(8,128)} %bitcast.8, f32[32,32]{1,0:T(8,128)} %refs_1_.3, f32[1,32]{1,0:T(1,128)} %bitcast.13, f32[3,3,16,64]{3,2,1,0:T(8,128)} %refs_3_.3, f32[3,32,64]{2,1,0:T(8,128)} %refs_4_.3, f32[3,32,64]{2,1,0:T(8,128)} %bitcast.10, ...), custom_call_target="tpu_custom_call" | custom-call | flops 10000000000 | bytes 10000000 | tf_op jit(solution)/shard_map/part_b/pallas_call | solution.py:825
  59.0 21.1 %part_c.1.red = f32[192,128]{1,0:T(8,128)} custom-call(f32[192,128]{1,0:T(8,128)} %get-tuple-element.32.refs_0_), custom_call_target="tpu_custom_call" | custom-call | flops 1000000 | bytes 10000000 | tf_op jit(solution)/shard_map/part_c/pallas_call | solution.py:825
  80.1 1.6 %unpack.1 = (f32[32,32]{1,0:T(8,128)}, f32[1,32]{1,0:T(1,128)}, f32[3,3,16,64]{3,2,1,0:T(8,128)}, f32[3,32,64]{2,1,0:T(8,128)}, f32[3,32,64]{2,1,0:T(8,128)}) custom-call(f32[192,128]{1,0:T(8,128)} %part_c.1.red), custom_call_target="tpu_custom_call" | custom-call | tf_op jit(solution)/shard_map/unpack/pallas_call | solution.py:850

commit v3 on v1

--- a/solution.py
+++ b/solution.py
@@ -71,17 +71,18 @@
         quad[z, z // 4] = 1
     quad = channel_eye(quad)
     xy0 = np.kron(b24, b24)
+    at4, at3 = (1, 2, 0, 3), (1, 0, 2)
     xy1 = np.zeros((256, 4, 4, 40))
     for j in range(4):
         for i in range(4):
             for r in range(36):
-                xy1[:, j, i, r] = np.kron(b24[:, i * 6 + r // 6], b24[:, j * 6 + r % 6])
+                xy1[:, j, i, r] = np.kron(b24[:, at4[i] * 6 + r // 6], b24[:, at4[j] * 6 + r % 6])
     xy2 = np.zeros((256, 368))
     for j in range(3):
         for i in range(3):
             for r in range(36):
                 xy2[:, (j * 3 + i) * 40 + r] = np.kron(
-                    b18[:, i * 6 + r // 6], b18[:, j * 6 + r % 6]
+                    b18[:, at3[i] * 6 + r // 6], b18[:, at3[j] * 6 + r % 6]
                 )
     z0 = channel_eye(b24.T)
     z1s, z2s = [], []
@@ -91,7 +92,8 @@
         if gz == 0:
             z1[12:18] = b24[:, 18:24].T
         else:
-            z1[14:20] = b24[:, 0:6].T
+            z1[12:16] = b24[:, 2:6].T
+            z1[16:18] = b24[:, 0:2].T
         z1s.append(right(channel_eye(z1)))
         z2 = np.zeros((16, 16))
         z2[0:6] = b18[:, 6:12].T
@@ -169,7 +171,7 @@
     result_hbm, red_ref = take(2)
     tab = dict(zip(NAMES, take(len(NAMES))))
     (feat, cot, result, fs, half, quart, hs, qs, kh, kl, pr, rh, rl, qh, ql, th, tl, bs, t12, pre, gs, gqh, gql, ghh, ghl,
-     wide, down, g12h, g12l, um, m2r, m0t, m1t, inw, outw, outt, skw, biast, gskip, gbias, pay, ra, rb, acc, red) = take(45)
+     wide, down, g12h, g12l, um, m2r, m0t, m1t, inw, outw, outt, skw, biast, gskip, gbias, pay, ra, rb, acc, red, zsend, zrecv, qth, qtl) = take(49)
     table_sem, local_sem, halo_send, halo_recv, red_send, red_recv = take(6)
 
     gx, gy, gz = lax.axis_index("gx"), lax.axis_index("gy"), lax.axis_index("gz")
@@ -206,31 +208,28 @@
 
     lax.fori_loop(1, group, greet_plane, 0)
 
-    @pl.when(gx == 0)
-    def _():
-        for j in (1, 2):
-            half[j, 0] = jnp.zeros((40, 640), F32)
-        quart[1, 0] = jnp.zeros((40, 512), F32)
-
-    @pl.when(gx == ngx - 1)
-    def _():
-        for j in (1, 2):
-            half[j, 3] = jnp.zeros((40, 640), F32)
-        quart[1, 2] = jnp.zeros((40, 512), F32)
-
-    @pl.when(gy == 0)
-    def _():
-        for i in range(4):
-            half[0, i] = jnp.zeros((40, 640), F32)
-        for i in range(3):
-            quart[0, i] = jnp.zeros((40, 512), F32)
-
-    @pl.when(gy == ngy - 1)
-    def _():
-        for i in range(4):
-            half[3, i] = jnp.zeros((40, 640), F32)
-        for i in range(3):
-            quart[2, i] = jnp.zeros((40, 512), F32)
+    def clear(j, i):
+        half[j, i] = jnp.zeros((40, 640), F32)
+
+    def clear_quarter(j, i):
+        quart[j, i] = jnp.zeros((40, 512), F32)
+
+    for edge, block in ((gx == 0, 2), (gx == ngx - 1, 3)):
+
+        @pl.when(edge)
+        def _():
+            clear(0, block)
+            clear(1, block)
+            clear_quarter(0, block - 1)
+
+    for edge, block in ((gy == 0, 2), (gy == ngy - 1, 3)):
+
+        @pl.when(edge)
+        def _():
+            for i in range(4):
+                clear(block, i)
+            for i in range(3):
+                clear_quarter(block - 1, i)
 
     load_f.wait()
     for name in NAMES[3:]:
@@ -252,10 +251,15 @@
         for j in range(2):
             for i in range(2):
                 r = (j * 2 + i) * 40
-                half[j + 1, i + 1, :, 128 * n : 128 * (n + 1)] = cells[r : r + 40]
+                half[j, i, :, 128 * n : 128 * (n + 1)] = cells[r : r + 40]
     loads["quad"].wait()
     cells = dot(lanes_cat(hi[160:208], lo[160:208]), tab["quad"][...])
-    quart[1, 1, :, 0:256] = cells[0:40]
+    quart[0, 0, :, 0:256] = cells[0:40]
+    for i in range(2):
+        a, b = half[0, i, :, 128:256], half[1, i, :, 128:256]
+        a = jnp.where(gz == 1, a, pltpu.roll(a, 64, 1))
+        b = jnp.where(gz == 1, pltpu.roll(b, 64, 1), b)
+        zsend[i] = jnp.where(iota((40, 128), 1) < 64, a, b)
 
     pl.semaphore_wait(barrier, ngy - 1 + group - 1)
 
@@ -269,38 +273,39 @@
             device_id_type=MESH,
         )
 
-    first = pl.multiple_of(128 * (1 - gz), 128)
-    own, far = pl.ds(0, 384), pl.ds(384, 256)
-    up_x, down_x = (gx + 1, gy, gz), (gx - 1, gy, gz)
-    up_y, down_y = (gx, gy + 1, gz), (gx, gy - 1, gz)
+    first = pl.multiple_of(256 * (1 - gz), 128)
+    own, far, qown, qfar = pl.ds(0, 384), pl.ds(384, 256), pl.ds(0, 256), pl.ds(256, 256)
+    mid, side = pl.ds(0, 2), pl.ds(2, 2)
+    qside = pl.ds(1, 2)
     across = (gx, gy, 1 - gz)
-    mid = pl.ds(1, 2)
-    z_half = remote(0, half.at[mid, mid, :, pl.ds(first, 256)], half.at[mid, mid, :, far], across)
-    z_quart = remote(1, quart.at[1, 1, :, pl.ds(0, 256)], quart.at[1, 1, :, pl.ds(256, 256)], across)
-    x_up = [
-        remote(2, half.at[mid, 2, :, own], half.at[mid, 0, :, own], up_x),
-        remote(3, half.at[mid, 2, :, far], half.at[mid, 0, :, far], up_x),
-        remote(4, quart.at[1, 1], quart.at[1, 0], up_x),
+    z_all = [
+        remote(0, half.at[mid, mid, :, pl.ds(first, 128)], half.at[mid, mid, :, pl.ds(384, 128)], across),
+        remote(1, zsend, zrecv, across),
+        remote(2, quart.at[0, 0, :, qown], quart.at[0, 0, :, qfar], across),
     ]
-    x_down = [
-        remote(5, half.at[mid, 1, :, own], half.at[mid, 3, :, own], down_x),
-        remote(6, half.at[mid, 1, :, far], half.at[mid, 3, :, far], down_x),
-        remote(7, quart.at[1, 1], quart.at[1, 2], down_x),
-    ]
-    y_up = [
-        remote(8, half.at[2, mid, :, own], half.at[0, mid, :, own], up_y),
-        remote(9, half.at[2, mid, :, far], half.at[0, mid, :, far], up_y),
-        remote(10, half.at[2, 0], half.at[0, 0], up_y),
-        remote(11, half.at[2, 3], half.at[0, 3], up_y),
-        remote(12, quart.at[1], quart.at[0], up_y),
-    ]
-    y_down = [
-        remote(13, half.at[1, mid, :, own], half.at[3, mid, :, own], down_y),
-        remote(14, half.at[1, mid, :, far], half.at[3, mid, :, far], down_y),
-        remote(15, half.at[1, 0], half.at[3, 0], down_y),
-        remote(16, half.at[1, 3], half.at[3, 3], down_y),
-        remote(17, quart.at[1], quart.at[2], down_y),
-    ]
+
+    def x_copies(k, src, dst, to):
+        return [
+            remote(k, half.at[mid, src, :, own], half.at[mid, dst, :, own], to),
+            remote(k + 1, quart.at[0, 0, :, qown], quart.at[0, dst - 1, :, qown], to),
+            remote(k + 2, half.at[mid, src, :, far], half.at[mid, dst, :, far], to),
+            remote(k + 3, quart.at[0, 0, :, qfar], quart.at[0, dst - 1, :, qfar], to),
+        ]
+
+    def y_copies(k, src, dst, to):
+        return [
+            remote(k, half.at[src, mid, :, own], half.at[dst, mid, :, own], to),
+            remote(k + 1, quart.at[0, 0, :, qown], quart.at[dst - 1, 0, :, qown], to),
+            remote(k + 2, half.at[src, side, :, own], half.at[dst, side, :, own], to),
+            remote(k + 3, quart.at[0, qside, :, qown], quart.at[dst - 1, qside, :, qown], to),
+            remote(k + 4, half.at[src, mid, :, far], half.at[dst, mid, :, far], to),
+            remote(k + 5, quart.at[0, 0, :, qfar], quart.at[dst - 1, 0, :, qfar], to),
+            remote(k + 6, half.at[src, side, :, far], half.at[dst, side, :, far], to),
+            remote(k + 7, quart.at[0, qside, :, qfar], quart.at[dst - 1, qside, :, qfar], to),
+        ]
+
+    xs = x_copies(3, 1, 2, (gx + 1, gy, gz)), x_copies(7, 0, 3, (gx - 1, gy, gz))
+    ys = y_copies(11, 1, 2, (gx, gy + 1, gz)), y_copies(19, 0, 3, (gx, gy - 1, gz))
 
     def each(copies, which, to_up, to_down, act):
         @pl.when(to_up)
@@ -314,15 +319,14 @@
                 act(copies[1][k])
 
     has_ux, has_dx, has_uy, has_dy = gx < ngx - 1, gx > 0, gy < ngy - 1, gy > 0
-    xs, ys = (x_up, x_down), (y_up, y_down)
     start = lambda c: c.start()
     recv = lambda c: c.wait_recv()
     sent = lambda c: c.wait_send()
 
-    z_half.start()
-    z_quart.start()
-    each(xs, (0,), has_ux, has_dx, start)
-    each(ys, (0,), has_uy, has_dy, start)
+    for c in z_all:
+        c.start()
+    each(xs, (0, 1), has_ux, has_dx, start)
+    each(ys, (0, 1), has_uy, has_dy, start)
 
     def dup64(x):
         eye = (iota((64, 128), 0) == iota((64, 128), 1) % 64).astype(BF)
@@ -432,18 +436,23 @@
     loads["xy0"].wait()
     xy_transform(tab["xy0"], fs, 576, 3, 256)
 
-    z_half.wait_recv()
-    z_quart.wait_recv()
-    each(xs, (1, 2), has_ux, has_dx, start)
-    each(ys, (1,), has_uy, has_dy, start)
+    each(xs, (0, 1), has_dx, has_ux, recv)
+    each(ys, (2, 3), has_uy, has_dy, start)
 
     loads["z0"].wait()
     z_transform(th[...], tl[...], tab["z0"], 768, kh, kl, 0)
+
+    for c in z_all:
+        c.wait_recv()
+    low = iota((40, 128), 1) < 64
+    for i in range(2):
+        a = zrecv[i]
+        half[0, i, :, 512:640] = jnp.where(low, a, 0.0)
+        half[1, i, :, 512:640] = jnp.where(low, pltpu.roll(a, 64, 1), 0.0)
+    each(xs, (2, 3), has_ux, has_dx, start)
+    each(ys, (4, 5), has_uy, has_dy, start)
+
     modes_forward(0)
-
-    each(xs, (0, 1, 2), has_dx, has_ux, recv)
-    each(ys, (2, 3, 4), has_uy, has_dy, start)
-
     loads["z0t"].wait()
     a = lanes_cat(qh[0], ql[0], qh[0])
     for n in range(3):
@@ -452,32 +461,49 @@
         hi, lo = split(dot(a, tz))
         bs[0:256, cols] = hi
         bs[256:512, cols] = lo
+    each(xs, (2, 3), has_dx, has_ux, recv)
+    each(ys, (6, 7), has_uy, has_dy, start)
     loads["inv"].wait()
     for n in range(3):
         cols = slice(256 * n, 256 * (n + 1))
         pre[:, cols] = pre[:, cols] + dot(tab["inv"][...], rows_cat(bs[0:512, cols], bs[0:256, cols]))
 
-    each(ys, (0, 1, 2, 3, 4), has_dy, has_uy, recv)
-    for j in range(4):
-        hi, lo = split(half[j].reshape(160, 640))
-        hs[160 * j : 160 * (j + 1)] = hi
-        hs[640 + 160 * j : 640 + 160 * (j + 1)] = lo
-    cells = rows_cat(quart[...].reshape(360, 512), jnp.zeros((8, 512), F32))
-    hi, lo = split(cells)
-    qs[0:368] = hi
-    qs[368:736] = lo
+    def halves_of(cols, qcols):
+        for j in range(4):
+            hi, lo = split(half[j, :, :, cols].reshape(160, -1))
+            hs[160 * j : 160 * (j + 1), cols] = hi
+            hs[640 + 160 * j : 640 + 160 * (j + 1), cols] = lo
+        cells = quart[:, :, :, qcols].reshape(360, 256)
+        hi, lo = split(rows_cat(cells, jnp.zeros((8, 256), F32)))
+        qs[0:368, qcols] = hi
+        qs[368:736, qcols] = lo
+
+    def one_chunk(table, data, rows, cols, into_h, into_l):
+        v = rows_cat(data[0 : 2 * rows, cols], data[0:rows, cols])
+        hi, lo = split(dot(table[...], v))
+        into_h[:, cols] = hi
+        into_l[:, cols] = lo
+
+    each(ys, (0, 1, 2, 3), has_dy, has_uy, recv)
+    halves_of(slice(0, 384), slice(0, 256))
     loads["xy1"].wait()
-    xy_transform(tab["xy1"], hs, 640, 2, 256)
-    data = rows_cat(hs[:, 512:640], hs[0:640, 512:640])
-    hi, lo = split(dot(tab["xy1"][...], data))
-    th[:, 512:640] = hi
-    tl[:, 512:640] = lo
+    loads["xy2"].wait()
+    one_chunk(tab["xy1"], hs, 640, slice(0, 256), th, tl)
+    v = lanes_cat(hs[0:640, 256:384], hs[640:1280, 256:384])
+    v = dot(tab["xy1"][:, 640:1920], rows_cat(v, v))
+    hi, lo = split(v[:, 0:128] + v[:, 128:256])
+    th[:, 256:384] = hi
+    tl[:, 256:384] = lo
+    one_chunk(tab["xy2"], qs, 368, slice(0, 256), qth, qtl)
+
+    each(ys, (4, 5, 6, 7), has_dy, has_uy, recv)
+    halves_of(slice(384, 640), slice(256, 512))
+    one_chunk(tab["xy1"], hs, 640, slice(384, 640), th, tl)
+    one_chunk(tab["xy2"], qs, 368, slice(256, 512), qth, qtl)
     loads["z1"].wait()
     z_transform(th[:, 0:640], tl[:, 0:640], tab["z1"], 640, kh, kl, 1)
-    loads["xy2"].wait()
-    xy_transform(tab["xy2"], qs, 368, 2, 256)
     loads["z2"].wait()
-    z_transform(th[:, 0:512], tl[:, 0:512], tab["z2"], 512, kh, kl, 2)
+    z_transform(qth[...], qtl[...], tab["z2"], 512, kh, kl, 2)
     lax.fori_loop(1, 3, lambda l, c: (modes_forward(l), c)[1], 0)
 
     loads["z1c"].wait()
@@ -663,10 +689,10 @@
     pushes(ngy, scatter, sent)
     pushes(group, exchange, sent)
     pushes(ngy, gather, sent)
-    z_half.wait_send()
-    z_quart.wait_send()
-    each(xs, (0, 1, 2), has_ux, has_dx, sent)
-    each(ys, (0, 1, 2, 3, 4), has_uy, has_dy, sent)
+    for c in z_all:
+        c.wait_send()
+    each(xs, range(4), has_ux, has_dx, sent)
+    each(ys, range(8), has_uy, has_dy, sent)
     store.wait()
 
 
@@ -746,10 +772,14 @@
         pltpu.VMEM((group, size, 128), F32),
         pltpu.VMEM((size, 128), F32),
         pltpu.VMEM((PAY, 128), F32),
+        pltpu.VMEM((2, 40, 128), F32),
+        pltpu.VMEM((2, 40, 128), F32),
+        pltpu.VMEM((256, 512), BF),
+        pltpu.VMEM((256, 512), BF),
         pltpu.SemaphoreType.DMA((len(NAMES),)),
         pltpu.SemaphoreType.DMA((3,)),
-        pltpu.SemaphoreType.DMA((18,)),
-        pltpu.SemaphoreType.DMA((18,)),
+        pltpu.SemaphoreType.DMA((27,)),
+        pltpu.SemaphoreType.DMA((27,)),
         pltpu.SemaphoreType.DMA((2 * ngy + group,)),
         pltpu.SemaphoreType.DMA((2 * ngy + group,)),
     ]

time: 70.2 us -> 62.1 us (0.88)
  Pallas kernels: 69.1 us -> 61.2 us
    pallas_call x1, Pallas kernels: 65.3 us -> 57.4 us  [per_device(): pl.pallas_call(lambda *refs: layer_kernel(sizes, *refs), name='layer', ou...]
where the time goes in v3:
time: 62.1 us; the launch traced here: 61.9 us
  Pallas kernels  61.2 us (99%)
  between operations  0.64 us (1%)
    pallas_call x1, Pallas kernels, per_device(): pl.pallas_call(lambda *refs: layer_kernel(sizes, *refs), name='layer', ou...  57.4 us
    pallas_call x1, Pallas kernels, per_device(): pl.pallas_call(unpack_kernel, name='unpack', out_shape=(jax.ShapeDtypeStr...  3.85 us

profile of v3, /device:TPU:1, one launch (start us, length us, event | category | flops | bytes accessed | tf_op | source)
XLA Modules:
  0.0 61.9 jit_solution(95942308962929326)
XLA Ops:
  0.6 57.4 %layer.1 = (f32[576,768]{1,0:T(8,128)}, f32[192,128]{1,0:T(8,128)}) custom-call(f32[576,768]{1,0:T(8,128)} %bitcast.7, f32[576,768]{1,0:T(8,128)} %bitcast.8, f32[32,32]{1,0:T(8,128)} %refs_2_.1, f32[1,32]{1,0:T(1,128)} %bitcast.12, f32[3,3,16,64]{3,2,1,0:T(8,128)} %refs_4_.1, f32[3,32,64]{2,1,0:T(8,128)} %refs_5_.1, f32[3,32,64]{2,1,0:T(8,128)} %bitcast.10, ...), custom_call_target="tpu_custom_call" | custom-call | flops 32000000000 | bytes 20000000 | tf_op jit(solution)/shard_map/layer/pallas_call | solution.py:789
  58.0 3.8 %unpack.1 = (f32[576,768]{1,0:T(8,128)}, f32[32,32]{1,0:T(8,128)}, f32[1,32]{1,0:T(1,128)}, f32[3,3,16,64]{3,2,1,0:T(8,128)}, f32[3,32,64]{2,1,0:T(8,128)}, /*index=5*/f32[3,32,64]{2,1,0:T(8,128)}) custom-call(f32[576,768]{1,0:T(8,128)} %get-tuple-element.14.result_in, f32[192,128]{1,0:T(8,128)} %get-tuple-element.15.red), custom_call_target="tpu_custom_call" | custom-call | tf_op jit(solution)/shard_map/unpack/pallas_call | solution.py:810

commit v4 on v3

--- a/solution.py
+++ b/solution.py
@@ -166,12 +166,14 @@
     ngx, ngy, ngz = sizes
     refs = list(refs)
     take = lambda n: [refs.pop(0) for _ in range(n)]
-    feat_hbm, cot_hbm, skip_ref, bias_ref, modes_ref, in_ref, out_ref = take(7)
+    feat_hbm, cot_hbm = take(2)
+    weights_hbm = take(5)
     hbm = dict(zip(NAMES, take(len(NAMES))))
-    result_hbm, red_ref = take(2)
+    result_hbm, red_hbm = take(2)
     tab = dict(zip(NAMES, take(len(NAMES))))
     (feat, cot, result, fs, half, quart, hs, qs, kh, kl, pr, rh, rl, qh, ql, th, tl, bs, t12, pre, gs, gqh, gql, ghh, ghl,
-     wide, down, g12h, g12l, um, m2r, m0t, m1t, inw, outw, outt, skw, biast, gskip, gbias, pay, ra, rb, acc, red, zsend, zrecv, qth, qtl) = take(49)
+     wide, down, g12h, g12l, um, m2r, m0t, m1t, inw, outw, outt, skw, biast, gskip, gbias, pay, ra, rb, acc, red, zsend, zrecv, qth, qtl, fst, kt,
+     skip_ref, bias_ref, modes_ref, in_ref, out_ref) = take(56)
     table_sem, local_sem, halo_send, halo_recv, red_send, red_recv = take(6)
 
     gx, gy, gz = lax.axis_index("gx"), lax.axis_index("gy"), lax.axis_index("gz")
@@ -188,6 +190,12 @@
         loads[name] = pltpu.make_async_copy(src, tab[name], table_sem.at[k])
         if k < 3:
             loads[name].start()
+    load_w = [
+        pltpu.make_async_copy(src, dst, local_sem.at[3 + k])
+        for k, (src, dst) in enumerate(zip(weights_hbm, (skip_ref, bias_ref, modes_ref, in_ref, out_ref)))
+    ]
+    for c in load_w:
+        c.start()
 
     barrier = pltpu.get_barrier_semaphore()
 
@@ -328,6 +336,9 @@
     each(xs, (0, 1), has_ux, has_dx, start)
     each(ys, (0, 1), has_uy, has_dy, start)
 
+    for c in load_w:
+        c.wait()
+
     def dup64(x):
         eye = (iota((64, 128), 0) == iota((64, 128), 1) % 64).astype(BF)
         return dot(x, eye)
@@ -411,6 +422,7 @@
 
     def modes_forward(l):
         data = [(kh[l, :, c], kl[l, :, c]) for c, _ in quads]
+        kt[l] = jnp.transpose(rows_cat(*[lanes_cat(a, b) for a, b in data]))
         p = dot(rows_cat(*[lanes_cat(a, b, a) for a, b in data]), inw[l])
         u = um[l]
         u = lanes_cat(u, u)
@@ -429,7 +441,9 @@
             qh[l, :, cols] = a
             ql[l, :, cols] = b
 
-    v = dot(stacked(fs), skw[...])
+    v = stacked(fs)
+    fst[...] = jnp.transpose(v)
+    v = dot(v, skw[...])
     v = v[:, 0:128] + v[:, 128:256] + biast[0:1]
     for n in range(6):
         pre[:, 128 * n : 128 * (n + 1)] = v[576 * n : 576 * (n + 1)]
@@ -567,21 +581,17 @@
     z_transform(g12h[0:256], g12l[0:256], tab["z1"], 384, gqh, gql, 1, (0, 640))
     z_transform(g12h[256:512], g12l[256:512], tab["z2ct"], 384, gqh, gql, 2)
 
-    total = dot(stacked(fs), stacked(gs), TN)
+    total = dot(fst[...], stacked(gs))
     total = total[0:128] + total[128:256]
     total = jnp.where(diag_io, total[:, 0:128] + total[:, 128:256], 0.0)
     s = total[0:32] + total[32:64] + total[64:96] + total[96:128]
     s = s + pltpu.roll(s, 64, 1)
     gskip[...] = s + pltpu.roll(s, 32, 1)
 
-    def gram(ah, al, bh, bl):
-        a, b = [], []
-        for ca, cb in quads:
-            x, y = ah[:, ca], al[:, ca]
-            v, w = bh[:, cb], bl[:, cb]
-            a += [x, y, x]
-            b += [v, v, w]
-        g = jnp.where(diag_ir, dot(rows_cat(*a), rows_cat(*b), TN), 0.0)
+    def gram(at, bh, bl):
+        g = dot(at, rows_cat(*[lanes_cat(bh[:, c], bl[:, c]) for _, c in quads]))
+        g = g[0:128] + g[128:256]
+        g = jnp.where(diag_ir, g[:, 0:256] + g[:, 256:512], 0.0)
         return fold_lanes(g[0:32] + g[32:64] + g[64:96] + g[96:128])
 
     low = iota((32, 128), 1) < 64
@@ -591,8 +601,8 @@
         u = lanes_cat(u, u)
         e = jnp.zeros((256, 128), F32)
         g2 = []
-        g_out = gram(gqh.at[l], gql.at[l], rh.at[l], rl.at[l])
         data = [(gqh[l, :, c], gql[l, :, c]) for c, _ in quads]
+        g_out = gram(jnp.transpose(rows_cat(*[lanes_cat(a, b) for a, b in data])), rh.at[l], rl.at[l])
         g = dot(rows_cat(*[lanes_cat(a, b, a) for a, b in data]), outt[l])
         for k, (_, cols) in enumerate(quads):
             gr = g[256 * k : 256 * (k + 1)]
@@ -604,7 +614,7 @@
             hi, lo = split(gr * (u * m2))
             rh[l, :, cols] = hi
             rl[l, :, cols] = lo
-        g_in = gram(kh.at[l], kl.at[l], rh.at[l], rl.at[l])
+        g_in = gram(kt[l], rh.at[l], rl.at[l])
         e = (e + pltpu.roll(e, 64, 1)).reshape(16, 16, 128)
         g0 = jnp.sum(e * m1t[l][None, :, :], axis=1)
         g1 = jnp.sum(e * m0t[l][:, None, :], axis=0)
@@ -684,7 +694,8 @@
     red[mine] = total
     pushes(ngy, gather, start)
     pushes(ngy, gather, recv)
-    red_ref[...] = red[...]
+    store_red = pltpu.make_async_copy(red, red_hbm, local_sem.at[8])
+    store_red.start()
 
     pushes(ngy, scatter, sent)
     pushes(group, exchange, sent)
@@ -694,14 +705,21 @@
     each(xs, range(4), has_ux, has_dx, sent)
     each(ys, range(8), has_uy, has_dy, sent)
     store.wait()
-
-
-def unpack_kernel(result_in, red, result_out, skip, bias, modes, fin, fout, held, sem):
-    parts = [pl.ds(144 * k, 144) for k in range(4)]
+    store_red.wait()
+
+
+def unpack_kernel(result_in, red_in, result_out, *refs):
+    outs, (red, held), bufs, sem = refs[0:5], refs[5:7], refs[7:12], refs[12]
+    skip, bias, modes, fin, fout = bufs
+    parts = [pl.ds(96 * k, 96) for k in range(6)]
+    fetch_red = pltpu.make_async_copy(red_in, red, sem.at[17])
+    fetch_red.start()
     fetch = [pltpu.make_async_copy(result_in.at[p], held.at[p], sem.at[k]) for k, p in enumerate(parts)]
-    store = [pltpu.make_async_copy(held.at[p], result_out.at[p], sem.at[4 + k]) for k, p in enumerate(parts)]
+    store = [pltpu.make_async_copy(held.at[p], result_out.at[p], sem.at[6 + k]) for k, p in enumerate(parts)]
+    small = [pltpu.make_async_copy(b, o, sem.at[12 + k]) for k, (b, o) in enumerate(zip(bufs, outs))]
     for copy in fetch:
         copy.start()
+    fetch_red.wait()
     skip[0:16] = red[48:64, 64:96]
     skip[16:32] = red[48:64, 96:128]
     bias[...] = red[112:113, 64:96]
@@ -712,10 +730,12 @@
         modes[l, 0] = red[row + 32 : row + 48, 0:64]
         modes[l, 1] = red[row + 32 : row + 48, 64:128]
         modes[l, 2] = red[row + 48 : row + 64, 0:64]
+    for copy in small:
+        copy.start()
     for a, b in zip(fetch, store):
         a.wait()
         b.start()
-    for copy in store:
+    for copy in store + small:
         copy.wait()
 
 
@@ -725,7 +745,6 @@
     group = ngx * ngz
     size = PAY // ngy
     any_spec = pl.BlockSpec(memory_space=pl.ANY)
-    vmem_spec = pl.BlockSpec(memory_space=pltpu.VMEM)
     scratch = [pltpu.VMEM(table_shape(n), BF) for n in NAMES] + [
         pltpu.VMEM((576, 768), F32),
         pltpu.VMEM((576, 768), F32),
@@ -776,8 +795,15 @@
         pltpu.VMEM((2, 40, 128), F32),
         pltpu.VMEM((256, 512), BF),
         pltpu.VMEM((256, 512), BF),
+        pltpu.VMEM((256, 3456), BF),
+        pltpu.VMEM((3, 256, 1024), BF),
+        pltpu.VMEM((CH, CH), F32),
+        pltpu.VMEM((1, CH), F32),
+        pltpu.VMEM((3, 3, MD, RK), F32),
+        pltpu.VMEM((3, CH, RK), F32),
+        pltpu.VMEM((3, CH, RK), F32),
         pltpu.SemaphoreType.DMA((len(NAMES),)),
-        pltpu.SemaphoreType.DMA((3,)),
+        pltpu.SemaphoreType.DMA((9,)),
         pltpu.SemaphoreType.DMA((27,)),
         pltpu.SemaphoreType.DMA((27,)),
         pltpu.SemaphoreType.DMA((2 * ngy + group,)),
@@ -790,8 +816,8 @@
             lambda *refs: layer_kernel(sizes, *refs),
             name="layer",
             out_shape=(jax.ShapeDtypeStruct((576, 768), F32), jax.ShapeDtypeStruct((PAY, 128), F32)),
-            in_specs=[any_spec] * 2 + [vmem_spec] * 5 + [any_spec] * len(NAMES),
-            out_specs=(any_spec, vmem_spec),
+            in_specs=[any_spec] * (7 + len(NAMES)),
+            out_specs=(any_spec, any_spec),
             scratch_shapes=scratch,
             compiler_params=pltpu.CompilerParams(
                 collective_id=0, has_side_effects=True, vmem_limit_bytes=60 * 1024 * 1024
@@ -818,9 +844,18 @@
                 jax.ShapeDtypeStruct((3, CH, RK), F32),
                 jax.ShapeDtypeStruct((3, CH, RK), F32),
             ),
-            in_specs=[any_spec, vmem_spec],
-            out_specs=(any_spec,) + (vmem_spec,) * 5,
-            scratch_shapes=[pltpu.VMEM((576, 768), F32), pltpu.SemaphoreType.DMA((8,))],
+            in_specs=[any_spec] * 2,
+            out_specs=(any_spec,) * 6,
+            scratch_shapes=[
+                pltpu.VMEM((PAY, 128), F32),
+                pltpu.VMEM((576, 768), F32),
+                pltpu.VMEM((CH, CH), F32),
+                pltpu.VMEM((1, CH), F32),
+                pltpu.VMEM((3, 3, MD, RK), F32),
+                pltpu.VMEM((3, CH, RK), F32),
+                pltpu.VMEM((3, CH, RK), F32),
+                pltpu.SemaphoreType.DMA((18,)),
+            ],
         )(result, red)
         return (outs[0].reshape(NP, NP, NP * CH), outs[1], outs[2].reshape(CH), outs[3], outs[4], jnp.swapaxes(outs[5], 1, 2))
 

time: 62.1 us -> 60.3 us (0.971)
  Pallas kernels: 61.2 us -> 59.5 us
    pallas_call x1, Pallas kernels: 3.85 us -> 2.39 us  [per_device(): pl.pallas_call(unpack_kernel, name='unpack', out_shape=(jax.ShapeDtypeStr...]
where the time goes in v4:
time: 60.3 us; the launch traced here: 60.2 us
  Pallas kernels  59.5 us (99%)
  between operations  0.64 us (1%)
    pallas_call x1, Pallas kernels, per_device(): pl.pallas_call(lambda *refs: layer_kernel(sizes, *refs), name='layer', ou...  57.1 us
    pallas_call x1, Pallas kernels, per_device(): pl.pallas_call(unpack_kernel, name='unpack', out_shape=(jax.ShapeDtypeStr...  2.39 us

profile of v4, /device:TPU:1, one launch (start us, length us, event | category | flops | bytes accessed | tf_op | source)
XLA Modules:
  0.0 60.2 jit_solution(14949444035074895379)
XLA Ops:
  0.6 57.1 %layer.1 = (f32[576,768]{1,0:T(8,128)}, f32[192,128]{1,0:T(8,128)}) custom-call(f32[576,768]{1,0:T(8,128)} %bitcast.7, f32[576,768]{1,0:T(8,128)} %bitcast.8, f32[32,32]{1,0:T(8,128)} %refs_2_.1, f32[1,32]{1,0:T(1,128)} %bitcast.12, f32[3,3,16,64]{3,2,1,0:T(8,128)} %refs_4_.1, f32[3,32,64]{2,1,0:T(8,128)} %refs_5_.1, f32[3,32,64]{2,1,0:T(8,128)} %bitcast.10, ...), custom_call_target="tpu_custom_call" | custom-call | flops 32000000000 | bytes 20000000 | tf_op jit(solution)/shard_map/layer/pallas_call | solution.py:815
  57.8 2.4 %unpack.1 = (f32[576,768]{1,0:T(8,128)}, f32[32,32]{1,0:T(8,128)}, f32[1,32]{1,0:T(1,128)}, f32[3,3,16,64]{3,2,1,0:T(8,128)}, f32[3,32,64]{2,1,0:T(8,128)}, /*index=5*/f32[3,32,64]{2,1,0:T(8,128)}) custom-call(f32[576,768]{1,0:T(8,128)} %get-tuple-element.14.result_in, f32[192,128]{1,0:T(8,128)} %get-tuple-element.15.red_in), custom_call_target="tpu_custom_call" | custom-call | tf_op jit(solution)/shard_map/unpack/pallas_call | solution.py:836

commit v5 on v4

--- a/solution.py
+++ b/solution.py
@@ -172,8 +172,8 @@
     result_hbm, red_hbm = take(2)
     tab = dict(zip(NAMES, take(len(NAMES))))
     (feat, cot, result, fs, half, quart, hs, qs, kh, kl, pr, rh, rl, qh, ql, th, tl, bs, t12, pre, gs, gqh, gql, ghh, ghl,
-     wide, down, g12h, g12l, um, m2r, m0t, m1t, inw, outw, outt, skw, biast, gskip, gbias, pay, ra, rb, acc, red, zsend, zrecv, qth, qtl, fst, kt,
-     skip_ref, bias_ref, modes_ref, in_ref, out_ref) = take(56)
+     wide, down, g12h, g12l, um, m2r, m0t, m1t, inw, outw, outt, skw, biast, gskip, gbias, pay, ra, rb, acc, red, zsend, zrecv, qth, qtl, fst, kt, kown,
+     skip_ref, bias_ref, modes_ref, in_ref, out_ref) = take(57)
     table_sem, local_sem, halo_send, halo_recv, red_send, red_recv = take(6)
 
     gx, gy, gz = lax.axis_index("gx"), lax.axis_index("gy"), lax.axis_index("gz")
@@ -510,15 +510,27 @@
     tl[:, 256:384] = lo
     one_chunk(tab["xy2"], qs, 368, slice(0, 256), qth, qtl)
 
+    def z_product(hi, lo, table, first, rows, depth):
+        tz = table[first : first + depth]
+        return dot(lanes_cat(hi, lo, hi), rows_cat(tz, tz, table[rows + first : rows + first + depth]))
+
+    loads["z1"].wait()
+    loads["z2"].wait()
+    kown[0] = z_product(th[:, 0:384], tl[:, 0:384], tab["z1"], 0, 640, 384)
+    kown[1] = z_product(qth[:, 0:256], qtl[:, 0:256], tab["z2"], 0, 512, 256)
+
     each(ys, (4, 5, 6, 7), has_dy, has_uy, recv)
     halves_of(slice(384, 640), slice(256, 512))
     one_chunk(tab["xy1"], hs, 640, slice(384, 640), th, tl)
     one_chunk(tab["xy2"], qs, 368, slice(256, 512), qth, qtl)
-    loads["z1"].wait()
-    z_transform(th[:, 0:640], tl[:, 0:640], tab["z1"], 640, kh, kl, 1)
-    loads["z2"].wait()
-    z_transform(qth[...], qtl[...], tab["z2"], 512, kh, kl, 2)
-    lax.fori_loop(1, 3, lambda l, c: (modes_forward(l), c)[1], 0)
+    hi, lo = split(kown[0] + z_product(th[:, 384:640], tl[:, 384:640], tab["z1"], 384, 640, 256))
+    kh[1] = hi
+    kl[1] = lo
+    hi, lo = split(kown[1] + z_product(qth[:, 256:512], qtl[:, 256:512], tab["z2"], 256, 512, 256))
+    kh[2] = hi
+    kl[2] = lo
+    for l in (1, 2):
+        modes_forward(l)
 
     loads["z1c"].wait()
     loads["z2c"].wait()
@@ -621,13 +633,14 @@
         g2 = jnp.sum(lanes_cat(*g2), axis=0, keepdims=True)
         g2 = jnp.where(iota((16, 1024), 0) == iota((16, 1024), 1) // 64, g2, 0.0)
         g2 = fold_lanes(g2)
-        row = pl.multiple_of(l * 64, 64)
+        row = 64 * l
         pay[pl.ds(row, 32), :] = jnp.where(low, g_in, g_out)
         pay[pl.ds(row + 32, 16), :] = jnp.where(low[0:16], g0, g1)
         pay[pl.ds(row + 48, 16), :] = jnp.where(low[0:16], g2, 0.0)
         return carry
 
-    lax.fori_loop(0, 3, modes_backward, 0)
+    for l in range(3):
+        modes_backward(l, 0)
     s = gskip[...]
     s = jnp.where(iota((16, 128), 1) < 96, s[0:16], s[16:32])
     pay[48:64] = jnp.where(low[0:16], pay[48:64], s)
@@ -679,20 +692,23 @@
             device_id_type=MESH,
         )
 
-    pushes(ngy, scatter, start)
+    for k in range(1, ngy):
+        scatter(k).start()
     pushes(ngy, scatter, recv)
     total = pay[mine]
     for k in range(1, ngy):
         total = total + ra[k]
     acc[...] = total
     rb[me] = total
-    pushes(group, exchange, start)
+    for k in range(1, group):
+        exchange(k).start()
     pushes(group, exchange, recv)
     total = rb[0]
     for k in range(1, group):
         total = total + rb[k]
     red[mine] = total
-    pushes(ngy, gather, start)
+    for k in range(1, ngy):
+        gather(k).start()
     pushes(ngy, gather, recv)
     store_red = pltpu.make_async_copy(red, red_hbm, local_sem.at[8])
     store_red.start()
@@ -797,6 +813,7 @@
         pltpu.VMEM((256, 512), BF),
         pltpu.VMEM((256, 3456), BF),
         pltpu.VMEM((3, 256, 1024), BF),
+        pltpu.VMEM((2, 256, 512), F32),
         pltpu.VMEM((CH, CH), F32),
         pltpu.VMEM((1, CH), F32),
         pltpu.VMEM((3, 3, MD, RK), F32),

time: 60.3 us -> 56.9 us (0.944)
  Pallas kernels: 59.5 us -> 55.9 us
    pallas_call x1, Pallas kernels: 57.1 us -> 53.5 us  [per_device(): pl.pallas_call(lambda *refs: layer_kernel(sizes, *refs), name='layer', ou...]
where the time goes in v5:
time: 56.9 us; the launch traced here: 56.7 us
  Pallas kernels  55.9 us (98%)
  between operations  0.8 us (1%)
    pallas_call x1, Pallas kernels, per_device(): pl.pallas_call(lambda *refs: layer_kernel(sizes, *refs), name='layer', ou...  53.5 us
    pallas_call x1, Pallas kernels, per_device(): pl.pallas_call(unpack_kernel, name='unpack', out_shape=(jax.ShapeDtypeStr...  2.39 us

profile of v5, /device:TPU:1, one launch (start us, length us, event | category | flops | bytes accessed | tf_op | source)
XLA Modules:
  0.0 56.7 jit_solution(12436680102062018661)
XLA Ops:
  0.6 53.5 %layer.1 = (f32[576,768]{1,0:T(8,128)}, f32[192,128]{1,0:T(8,128)}) custom-call(f32[576,768]{1,0:T(8,128)} %bitcast.7, f32[576,768]{1,0:T(8,128)} %bitcast.8, f32[32,32]{1,0:T(8,128)} %refs_2_.1, f32[1,32]{1,0:T(1,128)} %bitcast.12, f32[3,3,16,64]{3,2,1,0:T(8,128)} %refs_4_.1, f32[3,32,64]{2,1,0:T(8,128)} %refs_5_.1, f32[3,32,64]{2,1,0:T(8,128)} %bitcast.10, ...), custom_call_target="tpu_custom_call" | custom-call | flops 32000000000 | bytes 20000000 | tf_op jit(solution)/shard_map/layer/pallas_call | solution.py:832
  54.2 2.4 %unpack.1 = (f32[576,768]{1,0:T(8,128)}, f32[32,32]{1,0:T(8,128)}, f32[1,32]{1,0:T(1,128)}, f32[3,3,16,64]{3,2,1,0:T(8,128)}, f32[3,32,64]{2,1,0:T(8,128)}, /*index=5*/f32[3,32,64]{2,1,0:T(8,128)}) custom-call(f32[576,768]{1,0:T(8,128)} %get-tuple-element.14.result_in, f32[192,128]{1,0:T(8,128)} %get-tuple-element.15.red_in), custom_call_target="tpu_custom_call" | custom-call | tf_op jit(solution)/shard_map/unpack/pallas_call | solution.py:853

commit v6 on v5

--- a/solution.py
+++ b/solution.py
@@ -390,7 +390,8 @@
         m2r[l] = jnp.broadcast_to(jnp.sum(line, axis=0, keepdims=True), (8, 1024))
         return carry
 
-    lax.fori_loop(0, 3, spread, 0)
+    for l in range(3):
+        spread(l, 0)
 
     hi, lo = split(feat[...])
     fs[0:576] = hi
@@ -519,6 +520,9 @@
     kown[0] = z_product(th[:, 0:384], tl[:, 0:384], tab["z1"], 0, 640, 384)
     kown[1] = z_product(qth[:, 0:256], qtl[:, 0:256], tab["z2"], 0, 512, 256)
 
+    for name in ("z1c", "z2c", "xy12", "unpair", "xy12t", "z2ct"):
+        loads[name].wait()
+    load_c.wait()
     each(ys, (4, 5, 6, 7), has_dy, has_uy, recv)
     halves_of(slice(384, 640), slice(256, 512))
     one_chunk(tab["xy1"], hs, 640, slice(384, 640), th, tl)
@@ -532,64 +536,57 @@
     for l in (1, 2):
         modes_forward(l)
 
-    loads["z1c"].wait()
-    loads["z2c"].wait()
     for l, name in ((1, "z1c"), (2, "z2c")):
         tz = tab[name]
         v = dot(lanes_cat(qh[l], ql[l], qh[l]), rows_cat(tz[0:512], tz[0:512], tz[512:1024]))
         hi, lo = split(v)
         t12[256 * (l - 1) : 256 * l] = hi
         t12[512 + 256 * (l - 1) : 512 + 256 * l] = lo
-    loads["xy12"].wait()
-    loads["unpair"].wait()
     s = dot(tab["xy12"][...], rows_cat(t12[...], t12[0:512]))
+
+    scale = 1.0 / math.sqrt(ngx * ngy * ngz * NP**3)
+    c0 = math.sqrt(2.0 / math.pi)
+    sums = []
     for n in range(3):
+        cols = slice(256 * n, 256 * (n + 1))
         hi, lo = split(s[:, 128 * n : 128 * (n + 1)])
         v = dot(lanes_cat(hi, lo), tab["unpair"][...])
         for k in range(2):
             for step in range(2):
                 wide[2 * n + k, pl.ds(step, 144, stride=2), :] = v[:, 128 * k : 128 * (k + 1)]
-
-    load_c.wait()
-    scale = 1.0 / math.sqrt(ngx * ngy * ngz * NP**3)
-    c0 = math.sqrt(2.0 / math.pi)
-    store = pltpu.make_async_copy(result, result_hbm, local_sem.at[2])
-
-    def activate(m, carry):
-        rows = pl.ds(pl.multiple_of(m * 48, 48), 48)
-        v = lanes_cat(*[wide[n, pl.ds(pl.multiple_of(m * 24, 24), 24), :] for n in range(6)])
-        x = pre[rows, :] + rows_cat(v, v)
-        x2 = x * x
-        t = jnp.tanh(c0 * (x * (1.0 + 0.044715 * x2)))
-        half_t = 0.5 * (1.0 + t)
-        result[rows, :] = x * half_t
-        slope = half_t + 0.5 * x * (1.0 - t * t) * (c0 * (1.0 + (3 * 0.044715) * x2))
-        g = cot[rows, :] * scale * slope
-        hi, lo = split(g)
-        gs[rows, :] = hi
-        gs[pl.ds(pl.multiple_of(576 + m * 48, 48), 48), :] = lo
-        g2 = g[0:24] + g[24:48]
-        for n in range(6):
-            down[n, pl.ds(pl.multiple_of(m * 24, 24), 24), :] = g2[:, 128 * n : 128 * (n + 1)]
-        return carry + jnp.sum(g.reshape(6, 8, 768), axis=0)
-
-    colsum = lax.fori_loop(0, 12, activate, jnp.zeros((8, 768), F32))
-    store.start()
-    gbias[...] = fold_lanes(colsum)
-
-    xy_transform(tab["xy0"], gs, 576, 3, 256)
-    z_transform(th[...], tl[...], tab["z0"], 768, gqh, gql, 0)
-    for n in range(3):
+        colsum = jnp.zeros((8, 256), F32)
+        for m in range(12):
+            rows, pair = slice(48 * m, 48 * (m + 1)), slice(24 * m, 24 * (m + 1))
+            v = lanes_cat(wide[2 * n, pair], wide[2 * n + 1, pair])
+            x = pre[rows, cols] + rows_cat(v, v)
+            x2 = x * x
+            t = jnp.tanh(x * (c0 + (c0 * 0.044715) * x2))
+            half_t = 0.5 + 0.5 * t
+            result[rows, cols] = x * half_t
+            slope = half_t + x * (1.0 - t * t) * (0.5 * c0 + (1.5 * c0 * 0.044715) * x2)
+            g = cot[rows, cols] * scale * slope
+            hi, lo = split(g)
+            gs[rows, cols] = hi
+            gs[576 + 48 * m : 576 + 48 * (m + 1), cols] = lo
+            g2 = g[0:24] + g[24:48]
+            down[2 * n, pair] = g2[:, 0:128]
+            down[2 * n + 1, pair] = g2[:, 128:256]
+            colsum = colsum + jnp.sum(g.reshape(6, 8, 256), axis=0)
+        sums.append(colsum)
+        one_chunk(tab["xy0"], gs, 576, cols, th, tl)
         v = [down[2 * n + k, pl.ds(0, 144, stride=2), :] + down[2 * n + k, pl.ds(1, 144, stride=2), :] for k in range(2)]
         hi, lo = split(lanes_cat(*v))
         hi, lo = split(dot(lanes_cat(hi, lo), tab["pair"][...]))
         ghh[:, 128 * n : 128 * (n + 1)] = hi
         ghl[:, 128 * n : 128 * (n + 1)] = lo
-    loads["xy12t"].wait()
+    store = pltpu.make_async_copy(result, result_hbm, local_sem.at[2])
+    store.start()
+    gbias[...] = fold_lanes(lanes_cat(*sums))
+
+    z_transform(th[...], tl[...], tab["z0"], 768, gqh, gql, 0)
     hi, lo = split(dot(tab["xy12t"][...], rows_cat(ghh[...], ghl[...], ghh[...])))
     g12h[...] = hi
     g12l[...] = lo
-    loads["z2ct"].wait()
     z_transform(g12h[0:256], g12l[0:256], tab["z1"], 384, gqh, gql, 1, (0, 640))
     z_transform(g12h[256:512], g12l[256:512], tab["z2ct"], 384, gqh, gql, 2)
 

time: 56.9 us -> 55.9 us (0.982)
  Pallas kernels: 55.9 us -> 55 us
    pallas_call x1, Pallas kernels: 53.5 us -> 52.6 us  [per_device(): pl.pallas_call(lambda *refs: layer_kernel(sizes, *refs), name='layer', ou...]
where the time goes in v6:
time: 55.9 us; the launch traced here: 55.8 us
  Pallas kernels  55 us (98%)
  between operations  0.8 us (1%)
    pallas_call x1, Pallas kernels, per_device(): pl.pallas_call(lambda *refs: layer_kernel(sizes, *refs), name='layer', ou...  52.6 us
    pallas_call x1, Pallas kernels, per_device(): pl.pallas_call(unpack_kernel, name='unpack', out_shape=(jax.ShapeDtypeStr...  2.39 us

profile of v6, /device:TPU:1, one launch (start us, length us, event | category | flops | bytes accessed | tf_op | source)
XLA Modules:
  0.0 55.8 jit_solution(18310597725505420074)
XLA Ops:
  0.6 52.6 %layer.1 = (f32[576,768]{1,0:T(8,128)}, f32[192,128]{1,0:T(8,128)}) custom-call(f32[576,768]{1,0:T(8,128)} %bitcast.7, f32[576,768]{1,0:T(8,128)} %bitcast.8, f32[32,32]{1,0:T(8,128)} %refs_2_.1, f32[1,32]{1,0:T(1,128)} %bitcast.12, f32[3,3,16,64]{3,2,1,0:T(8,128)} %refs_4_.1, f32[3,32,64]{2,1,0:T(8,128)} %refs_5_.1, f32[3,32,64]{2,1,0:T(8,128)} %bitcast.10, ...), custom_call_target="tpu_custom_call" | custom-call | flops 32000000000 | bytes 20000000 | tf_op jit(solution)/shard_map/layer/pallas_call | solution.py:829
  53.2 2.4 %unpack.1 = (f32[576,768]{1,0:T(8,128)}, f32[32,32]{1,0:T(8,128)}, f32[1,32]{1,0:T(1,128)}, f32[3,3,16,64]{3,2,1,0:T(8,128)}, f32[3,32,64]{2,1,0:T(8,128)}, /*index=5*/f32[3,32,64]{2,1,0:T(8,128)}) custom-call(f32[576,768]{1,0:T(8,128)} %get-tuple-element.14.result_in, f32[192,128]{1,0:T(8,128)} %get-tuple-element.15.red_in), custom_call_target="tpu_custom_call" | custom-call | tf_op jit(solution)/shard_map/unpack/pallas_call | solution.py:850

commit v7 on v6

--- a/solution.py
+++ b/solution.py
@@ -172,16 +172,21 @@
     result_hbm, red_hbm = take(2)
     tab = dict(zip(NAMES, take(len(NAMES))))
     (feat, cot, result, fs, half, quart, hs, qs, kh, kl, pr, rh, rl, qh, ql, th, tl, bs, t12, pre, gs, gqh, gql, ghh, ghl,
-     wide, down, g12h, g12l, um, m2r, m0t, m1t, inw, outw, outt, skw, biast, gskip, gbias, pay, ra, rb, acc, red, zsend, zrecv, qth, qtl, fst, kt, kown,
-     skip_ref, bias_ref, modes_ref, in_ref, out_ref) = take(57)
+     wide, down, g12h, g12l, um, m2r, m0t, m1t, inw, outw, outt, skw, biast, gskip, gbias, pay, ra, rb, acc, red, zsend, zrecv, qth, qtl, fst, kt, kown, strips, sh, sl,
+     skip_ref, bias_ref, modes_ref, in_ref, out_ref) = take(60)
     table_sem, local_sem, halo_send, halo_recv, red_send, red_recv = take(6)
 
     gx, gy, gz = lax.axis_index("gx"), lax.axis_index("gy"), lax.axis_index("gz")
     me = gx * ngz + gz
     group = ngx * ngz
 
-    load_f = pltpu.make_async_copy(feat_hbm, feat, local_sem.at[0])
-    load_f.start()
+    thirds = [slice(256 * n, 256 * (n + 1)) for n in range(3)]
+    load_f = [
+        pltpu.make_async_copy(feat_hbm.at[:, pl.ds(256 * n, 256)], feat.at[:, pl.ds(256 * n, 256)], local_sem.at[9 + n])
+        for n in range(3)
+    ]
+    for c in load_f:
+        c.start()
     load_c = pltpu.make_async_copy(cot_hbm, cot, local_sem.at[1])
     loads = {}
     for k, name in enumerate(NAMES):
@@ -239,30 +244,25 @@
             for i in range(3):
                 clear_quarter(block - 1, i)
 
-    load_f.wait()
-    for name in NAMES[3:]:
-        loads[name].start()
-        if name == "xy2":
-            load_c.start()
-    cells = feat[...].reshape(12, 2, 24, 768)
-    hi, lo = split((cells[:, 0] + cells[:, 1]).reshape(288, 768))
-    gs[0:288] = hi
-    gs[288:576] = lo
     loads["pool"].wait()
-    for n in range(3):
-        pre[0:208, 256 * n : 256 * (n + 1)] = dot(tab["pool"][...], gs[0:576, 256 * n : 256 * (n + 1)])
-    hi, lo = split(pre[0:208])
     loads["pair"].wait()
-    for n in range(3):
-        cols = slice(256 * n, 256 * (n + 1))
-        cells = dot(lanes_cat(hi[0:160, cols], lo[0:160, cols]), tab["pair"][...])
+    for n, cols in enumerate(thirds):
+        load_f[n].wait()
+        if n == 2:
+            for name in NAMES[3:]:
+                loads[name].start()
+                if name == "xy2":
+                    load_c.start()
+        cells = feat[:, cols].reshape(12, 2, 24, 256)
+        hi, lo = split((cells[:, 0] + cells[:, 1]).reshape(288, 256))
+        hi, lo = split(dot(tab["pool"][...], rows_cat(hi, lo)))
+        strips[0, :, cols] = hi[160:208]
+        strips[1, :, cols] = lo[160:208]
+        cells = dot(lanes_cat(hi[0:160], lo[0:160]), tab["pair"][...])
         for j in range(2):
             for i in range(2):
                 r = (j * 2 + i) * 40
                 half[j, i, :, 128 * n : 128 * (n + 1)] = cells[r : r + 40]
-    loads["quad"].wait()
-    cells = dot(lanes_cat(hi[160:208], lo[160:208]), tab["quad"][...])
-    quart[0, 0, :, 0:256] = cells[0:40]
     for i in range(2):
         a, b = half[0, i, :, 128:256], half[1, i, :, 128:256]
         a = jnp.where(gz == 1, a, pltpu.roll(a, 64, 1))
@@ -331,8 +331,12 @@
     recv = lambda c: c.wait_recv()
     sent = lambda c: c.wait_send()
 
-    for c in z_all:
-        c.start()
+    z_all[0].start()
+    z_all[1].start()
+    loads["quad"].wait()
+    cells = dot(lanes_cat(strips[0], strips[1]), tab["quad"][...])
+    quart[0, 0, :, 0:256] = cells[0:40]
+    z_all[2].start()
     each(xs, (0, 1), has_ux, has_dx, start)
     each(ys, (0, 1), has_uy, has_dy, start)
 
@@ -590,12 +594,13 @@
     z_transform(g12h[0:256], g12l[0:256], tab["z1"], 384, gqh, gql, 1, (0, 640))
     z_transform(g12h[256:512], g12l[256:512], tab["z2ct"], 384, gqh, gql, 2)
 
-    total = dot(fst[...], stacked(gs))
-    total = total[0:128] + total[128:256]
-    total = jnp.where(diag_io, total[:, 0:128] + total[:, 128:256], 0.0)
-    s = total[0:32] + total[32:64] + total[64:96] + total[96:128]
-    s = s + pltpu.roll(s, 64, 1)
-    gskip[...] = s + pltpu.roll(s, 32, 1)
+    def skip_gradient():
+        total = dot(fst[...], stacked(gs))
+        total = total[0:128] + total[128:256]
+        total = jnp.where(diag_io, total[:, 0:128] + total[:, 128:256], 0.0)
+        s = total[0:32] + total[32:64] + total[64:96] + total[96:128]
+        s = s + pltpu.roll(s, 64, 1)
+        gskip[...] = s + pltpu.roll(s, 32, 1)
 
     def gram(at, bh, bl):
         g = dot(at, rows_cat(*[lanes_cat(bh[:, c], bl[:, c]) for _, c in quads]))
@@ -605,14 +610,15 @@
 
     low = iota((32, 128), 1) < 64
 
-    def modes_backward(l, carry):
+    def rank_cotangents(l):
+        data = [(gqh[l, :, c], gql[l, :, c]) for c, _ in quads]
+        return dot(rows_cat(*[lanes_cat(a, b, a) for a, b in data]), outt[l])
+
+    def weigh(l, g):
         u = um[l]
         u = lanes_cat(u, u)
         e = jnp.zeros((256, 128), F32)
         g2 = []
-        data = [(gqh[l, :, c], gql[l, :, c]) for c, _ in quads]
-        g_out = gram(jnp.transpose(rows_cat(*[lanes_cat(a, b) for a, b in data])), rh.at[l], rl.at[l])
-        g = dot(rows_cat(*[lanes_cat(a, b, a) for a, b in data]), outt[l])
         for k, (_, cols) in enumerate(quads):
             gr = g[256 * k : 256 * (k + 1)]
             d = gr * pr[l, :, cols]
@@ -621,23 +627,33 @@
             e = e + dm[:, 0:128] + dm[:, 128:256]
             g2.append(jnp.sum((d * u).reshape(32, 8, 256), axis=0))
             hi, lo = split(gr * (u * m2))
-            rh[l, :, cols] = hi
-            rl[l, :, cols] = lo
-        g_in = gram(kt[l], rh.at[l], rl.at[l])
+            sh[l, :, cols] = hi
+            sl[l, :, cols] = lo
         e = (e + pltpu.roll(e, 64, 1)).reshape(16, 16, 128)
         g0 = jnp.sum(e * m1t[l][None, :, :], axis=1)
         g1 = jnp.sum(e * m0t[l][:, None, :], axis=0)
         g2 = jnp.sum(lanes_cat(*g2), axis=0, keepdims=True)
         g2 = jnp.where(iota((16, 1024), 0) == iota((16, 1024), 1) // 64, g2, 0.0)
-        g2 = fold_lanes(g2)
         row = 64 * l
-        pay[pl.ds(row, 32), :] = jnp.where(low, g_in, g_out)
-        pay[pl.ds(row + 32, 16), :] = jnp.where(low[0:16], g0, g1)
-        pay[pl.ds(row + 48, 16), :] = jnp.where(low[0:16], g2, 0.0)
-        return carry
-
-    for l in range(3):
-        modes_backward(l, 0)
+        pay[row + 32 : row + 48] = jnp.where(low[0:16], g0, g1)
+        pay[row + 48 : row + 64] = jnp.where(low[0:16], fold_lanes(g2), 0.0)
+
+    def factors(l):
+        data = [(gqh[l, :, c], gql[l, :, c]) for c, _ in quads]
+        g_out = gram(jnp.transpose(rows_cat(*[lanes_cat(a, b) for a, b in data])), rh.at[l], rl.at[l])
+        g_in = gram(kt[l], sh.at[l], sl.at[l])
+        pay[64 * l : 64 * l + 32] = jnp.where(low, g_in, g_out)
+
+    g0 = rank_cotangents(0)
+    g1 = rank_cotangents(1)
+    weigh(0, g0)
+    factors(0)
+    g2 = rank_cotangents(2)
+    weigh(1, g1)
+    factors(1)
+    weigh(2, g2)
+    skip_gradient()
+    factors(2)
     s = gskip[...]
     s = jnp.where(iota((16, 128), 1) < 96, s[0:16], s[16:32])
     pay[48:64] = jnp.where(low[0:16], pay[48:64], s)
@@ -811,13 +827,16 @@
         pltpu.VMEM((256, 3456), BF),
         pltpu.VMEM((3, 256, 1024), BF),
         pltpu.VMEM((2, 256, 512), F32),
+        pltpu.VMEM((2, 48, 768), BF),
+        pltpu.VMEM((3, 256, 1024), BF),
+        pltpu.VMEM((3, 256, 1024), BF),
         pltpu.VMEM((CH, CH), F32),
         pltpu.VMEM((1, CH), F32),
         pltpu.VMEM((3, 3, MD, RK), F32),
         pltpu.VMEM((3, CH, RK), F32),
         pltpu.VMEM((3, CH, RK), F32),
         pltpu.SemaphoreType.DMA((len(NAMES),)),
-        pltpu.SemaphoreType.DMA((9,)),
+        pltpu.SemaphoreType.DMA((12,)),
         pltpu.SemaphoreType.DMA((27,)),
         pltpu.SemaphoreType.DMA((27,)),
         pltpu.SemaphoreType.DMA((2 * ngy + group,)),

time: 55.9 us -> 55.4 us (level)
  Pallas kernels: 55 us -> 54.4 us
where the time goes in v7:
time: 55.4 us; the launch traced here: 55.2 us
  Pallas kernels  54.4 us (98%)
  between operations  0.8 us (1%)
    pallas_call x1, Pallas kernels, per_device(): pl.pallas_call(lambda *refs: layer_kernel(sizes, *refs), name='layer', ou...  52 us
    pallas_call x1, Pallas kernels, per_device(): pl.pallas_call(unpack_kernel, name='unpack', out_shape=(jax.ShapeDtypeStr...  2.39 us

profile of v7, /device:TPU:1, one launch (start us, length us, event | category | flops | bytes accessed | tf_op | source)
XLA Modules:
  0.0 55.2 jit_solution(8369774249250635602)
XLA Ops:
  0.6 52.0 %layer.1 = (f32[576,768]{1,0:T(8,128)}, f32[192,128]{1,0:T(8,128)}) custom-call(f32[576,768]{1,0:T(8,128)} %bitcast.7, f32[576,768]{1,0:T(8,128)} %bitcast.8, f32[32,32]{1,0:T(8,128)} %refs_2_.1, f32[1,32]{1,0:T(1,128)} %bitcast.12, f32[3,3,16,64]{3,2,1,0:T(8,128)} %refs_4_.1, f32[3,32,64]{2,1,0:T(8,128)} %refs_5_.1, f32[3,32,64]{2,1,0:T(8,128)} %bitcast.10, ...), custom_call_target="tpu_custom_call" | custom-call | flops 32000000000 | bytes 20000000 | tf_op jit(solution)/shard_map/layer/pallas_call | solution.py:848
  52.7 2.4 %unpack.1 = (f32[576,768]{1,0:T(8,128)}, f32[32,32]{1,0:T(8,128)}, f32[1,32]{1,0:T(1,128)}, f32[3,3,16,64]{3,2,1,0:T(8,128)}, f32[3,32,64]{2,1,0:T(8,128)}, /*index=5*/f32[3,32,64]{2,1,0:T(8,128)}) custom-call(f32[576,768]{1,0:T(8,128)} %get-tuple-element.14.result_in, f32[192,128]{1,0:T(8,128)} %get-tuple-element.15.red_in), custom_call_target="tpu_custom_call" | custom-call | tf_op jit(solution)/shard_map/unpack/pallas_call | solution.py:869

commit v8 on v7

--- a/solution.py
+++ b/solution.py
@@ -282,7 +282,8 @@
         )
 
     first = pl.multiple_of(256 * (1 - gz), 128)
-    own, far, qown, qfar = pl.ds(0, 384), pl.ds(384, 256), pl.ds(0, 256), pl.ds(256, 256)
+    own, full, rest = pl.ds(0, 384), pl.ds(384, 128), pl.ds(512, 128)
+    qown, qfar = pl.ds(0, 256), pl.ds(256, 256)
     mid, side = pl.ds(0, 2), pl.ds(2, 2)
     qside = pl.ds(1, 2)
     across = (gx, gy, 1 - gz)
@@ -296,8 +297,9 @@
         return [
             remote(k, half.at[mid, src, :, own], half.at[mid, dst, :, own], to),
             remote(k + 1, quart.at[0, 0, :, qown], quart.at[0, dst - 1, :, qown], to),
-            remote(k + 2, half.at[mid, src, :, far], half.at[mid, dst, :, far], to),
-            remote(k + 3, quart.at[0, 0, :, qfar], quart.at[0, dst - 1, :, qfar], to),
+            remote(k + 2, half.at[mid, src, :, full], half.at[mid, dst, :, full], to),
+            remote(k + 3, half.at[mid, src, :, rest], half.at[mid, dst, :, rest], to),
+            remote(k + 4, quart.at[0, 0, :, qfar], quart.at[0, dst - 1, :, qfar], to),
         ]
 
     def y_copies(k, src, dst, to):
@@ -306,14 +308,16 @@
             remote(k + 1, quart.at[0, 0, :, qown], quart.at[dst - 1, 0, :, qown], to),
             remote(k + 2, half.at[src, side, :, own], half.at[dst, side, :, own], to),
             remote(k + 3, quart.at[0, qside, :, qown], quart.at[dst - 1, qside, :, qown], to),
-            remote(k + 4, half.at[src, mid, :, far], half.at[dst, mid, :, far], to),
-            remote(k + 5, quart.at[0, 0, :, qfar], quart.at[dst - 1, 0, :, qfar], to),
-            remote(k + 6, half.at[src, side, :, far], half.at[dst, side, :, far], to),
-            remote(k + 7, quart.at[0, qside, :, qfar], quart.at[dst - 1, qside, :, qfar], to),
+            remote(k + 4, half.at[src, mid, :, full], half.at[dst, mid, :, full], to),
+            remote(k + 5, half.at[src, side, :, full], half.at[dst, side, :, full], to),
+            remote(k + 6, half.at[src, mid, :, rest], half.at[dst, mid, :, rest], to),
+            remote(k + 7, quart.at[0, 0, :, qfar], quart.at[dst - 1, 0, :, qfar], to),
+            remote(k + 8, half.at[src, side, :, rest], half.at[dst, side, :, rest], to),
+            remote(k + 9, quart.at[0, qside, :, qfar], quart.at[dst - 1, qside, :, qfar], to),
         ]
 
-    xs = x_copies(3, 1, 2, (gx + 1, gy, gz)), x_copies(7, 0, 3, (gx - 1, gy, gz))
-    ys = y_copies(11, 1, 2, (gx, gy + 1, gz)), y_copies(19, 0, 3, (gx, gy - 1, gz))
+    xs = x_copies(3, 1, 2, (gx + 1, gy, gz)), x_copies(8, 0, 3, (gx - 1, gy, gz))
+    ys = y_copies(13, 1, 2, (gx, gy + 1, gz)), y_copies(23, 0, 3, (gx, gy - 1, gz))
 
     def each(copies, which, to_up, to_down, act):
         @pl.when(to_up)
@@ -457,21 +461,27 @@
 
     each(xs, (0, 1), has_dx, has_ux, recv)
     each(ys, (2, 3), has_uy, has_dy, start)
+    z_all[0].wait_recv()
+    each(xs, (2,), has_ux, has_dx, start)
+    each(ys, (4,), has_uy, has_dy, start)
 
     loads["z0"].wait()
     z_transform(th[...], tl[...], tab["z0"], 768, kh, kl, 0)
 
-    for c in z_all:
+    for c in z_all[1:]:
         c.wait_recv()
     low = iota((40, 128), 1) < 64
     for i in range(2):
         a = zrecv[i]
         half[0, i, :, 512:640] = jnp.where(low, a, 0.0)
         half[1, i, :, 512:640] = jnp.where(low, pltpu.roll(a, 64, 1), 0.0)
-    each(xs, (2, 3), has_ux, has_dx, start)
-    each(ys, (4, 5), has_uy, has_dy, start)
+    each(xs, (3, 4), has_ux, has_dx, start)
+    each(ys, (6, 7), has_uy, has_dy, start)
 
     modes_forward(0)
+
+    each(xs, (2,), has_dx, has_ux, recv)
+    each(ys, (5,), has_uy, has_dy, start)
     loads["z0t"].wait()
     a = lanes_cat(qh[0], ql[0], qh[0])
     for n in range(3):
@@ -480,8 +490,8 @@
         hi, lo = split(dot(a, tz))
         bs[0:256, cols] = hi
         bs[256:512, cols] = lo
-    each(xs, (2, 3), has_dx, has_ux, recv)
-    each(ys, (6, 7), has_uy, has_dy, start)
+    each(xs, (3, 4), has_dx, has_ux, recv)
+    each(ys, (8, 9), has_uy, has_dy, start)
     loads["inv"].wait()
     for n in range(3):
         cols = slice(256 * n, 256 * (n + 1))
@@ -527,7 +537,7 @@
     for name in ("z1c", "z2c", "xy12", "unpair", "xy12t", "z2ct"):
         loads[name].wait()
     load_c.wait()
-    each(ys, (4, 5, 6, 7), has_dy, has_uy, recv)
+    each(ys, range(4, 10), has_dy, has_uy, recv)
     halves_of(slice(384, 640), slice(256, 512))
     one_chunk(tab["xy1"], hs, 640, slice(384, 640), th, tl)
     one_chunk(tab["xy2"], qs, 368, slice(256, 512), qth, qtl)
@@ -731,8 +741,8 @@
     pushes(ngy, gather, sent)
     for c in z_all:
         c.wait_send()
-    each(xs, range(4), has_ux, has_dx, sent)
-    each(ys, range(8), has_uy, has_dy, sent)
+    each(xs, range(5), has_ux, has_dx, sent)
+    each(ys, range(10), has_uy, has_dy, sent)
     store.wait()
     store_red.wait()
 
@@ -837,8 +847,8 @@
         pltpu.VMEM((3, CH, RK), F32),
         pltpu.SemaphoreType.DMA((len(NAMES),)),
         pltpu.SemaphoreType.DMA((12,)),
-        pltpu.SemaphoreType.DMA((27,)),
-        pltpu.SemaphoreType.DMA((27,)),
+        pltpu.SemaphoreType.DMA((33,)),
+        pltpu.SemaphoreType.DMA((33,)),
         pltpu.SemaphoreType.DMA((2 * ngy + group,)),
         pltpu.SemaphoreType.DMA((2 * ngy + group,)),
     ]

time: 55.4 us -> 56.1 us (1.013)
  Pallas kernels: 54.4 us -> 55.1 us
    pallas_call x1, Pallas kernels: 52 us -> 52.7 us  [per_device(): pl.pallas_call(lambda *refs: layer_kernel(sizes, *refs), name='layer', ou...]
where the time goes in v8:
time: 56.1 us; the launch traced here: 55.9 us
  Pallas kernels  55.1 us (98%)
  between operations  0.8 us (1%)
    pallas_call x1, Pallas kernels, per_device(): pl.pallas_call(lambda *refs: layer_kernel(sizes, *refs), name='layer', ou...  52.7 us
    pallas_call x1, Pallas kernels, per_device(): pl.pallas_call(unpack_kernel, name='unpack', out_shape=(jax.ShapeDtypeStr...  2.39 us

profile of v8, /device:TPU:1, one launch (start us, length us, event | category | flops | bytes accessed | tf_op | source)
XLA Modules:
  0.0 55.9 jit_solution(8902236896173157032)
XLA Ops:
  0.6 52.7 %layer.1 = (f32[576,768]{1,0:T(8,128)}, f32[192,128]{1,0:T(8,128)}) custom-call(f32[576,768]{1,0:T(8,128)} %bitcast.7, f32[576,768]{1,0:T(8,128)} %bitcast.8, f32[32,32]{1,0:T(8,128)} %refs_2_.1, f32[1,32]{1,0:T(1,128)} %bitcast.12, f32[3,3,16,64]{3,2,1,0:T(8,128)} %refs_4_.1, f32[3,32,64]{2,1,0:T(8,128)} %refs_5_.1, f32[3,32,64]{2,1,0:T(8,128)} %bitcast.10, ...), custom_call_target="tpu_custom_call" | custom-call | flops 32000000000 | bytes 20000000 | tf_op jit(solution)/shard_map/layer/pallas_call | solution.py:858
  53.4 2.4 %unpack.1 = (f32[576,768]{1,0:T(8,128)}, f32[32,32]{1,0:T(8,128)}, f32[1,32]{1,0:T(1,128)}, f32[3,3,16,64]{3,2,1,0:T(8,128)}, f32[3,32,64]{2,1,0:T(8,128)}, /*index=5*/f32[3,32,64]{2,1,0:T(8,128)}) custom-call(f32[576,768]{1,0:T(8,128)} %get-tuple-element.14.result_in, f32[192,128]{1,0:T(8,128)} %get-tuple-element.15.red_in), custom_call_target="tpu_custom_call" | custom-call | tf_op jit(solution)/shard_map/unpack/pallas_call | solution.py:879
